TPU v7x, 32 devices: a whole 2x2x4 slice. The times are simulated.
32 devices in a mesh: dp: 16 (over z, x, core), outer: 2 (over y).
Axes of the slice: x: 2, y: 2, z: 4, core: 2. Of those that a mesh axis runs over, the one named last changes fastest.
Arguments:
- clip_frames: bfloat16 [256, 4, 8, 8, 256], P(('dp', 'outer')), may hold values from -6 to 6
- valid_mask: int32 [256, 4, 8, 8], P(('dp', 'outer')), may hold values from 0 to 1, as said below
- labels: int32 [256], P(('dp', 'outer')), may hold values from 0 to 399
- clip_keep: int32 [256], P(('dp', 'outer')), may hold values from 0 to 1, as said below
- step_count: int32 [1], replicated, may hold values from 1 to 20
- w_entry: float32 [256, 512], P(None, ('dp', 'outer')), may hold values from -0.375 to 0.375
- w_spatial: float32 [9, 512, 1152], P(None, ('dp', 'outer')), may hold values from -0.09375 to 0.09375
- w_temporal: float32 [3, 1152, 512], P(None, None, ('dp', 'outer')), may hold values from -0.109375 to 0.109375
- w_head: float32 [512, 400], P(('dp', 'outer')), may hold values from -0.25 to 0.25
- small_params: float32 [3728], replicated, may hold values from 0.5 to 1.5
- entry_first: float32 [256, 512], P(None, ('dp', 'outer')), may hold values from -0.005859375 to 0.005859375
- entry_second: float32 [256, 512], P(None, ('dp', 'outer')), may hold values from 1.4424324e-07 to 5.76973e-07
- spatial_first: float32 [9, 512, 1152], P(None, ('dp', 'outer')), may hold values from -0.001953125 to 0.001953125
- spatial_second: float32 [9, 512, 1152], P(None, ('dp', 'outer')), may hold values from 1.9073486e-08 to 7.6293944e-08
- temporal_first: float32 [3, 1152, 512], P(None, None, ('dp', 'outer')), may hold values from -0.009765625 to 0.009765625
- temporal_second: float32 [3, 1152, 512], P(None, None, ('dp', 'outer')), may hold values from 4.7683716e-07 to 1.9073486e-06
- head_first: float32 [512, 400], P(('dp', 'outer')), may hold values from -0.0390625 to 0.0390625
- head_second: float32 [512, 400], P(('dp', 'outer')), may hold values from 6.25e-06 to 2.5e-05
- small_first: float32 [3728], replicated
- small_second: float32 [3728], replicated
Outputs:
- loss: float32 [], replicated
- entry_new: float32 [256, 512], P(None, ('dp', 'outer'))
- entry_first_new: float32 [256, 512], P(None, ('dp', 'outer'))
- entry_second_new: float32 [256, 512], P(None, ('dp', 'outer'))
- spatial_new: float32 [9, 512, 1152], P(None, ('dp', 'outer'))
- spatial_first_new: float32 [9, 512, 1152], P(None, ('dp', 'outer'))
- spatial_second_new: float32 [9, 512, 1152], P(None, ('dp', 'outer'))
- temporal_new: float32 [3, 1152, 512], P(None, None, ('dp', 'outer'))
- temporal_first_new: float32 [3, 1152, 512], P(None, None, ('dp', 'outer'))
- temporal_second_new: float32 [3, 1152, 512], P(None, None, ('dp', 'outer'))
- head_new: float32 [512, 400], P(('dp', 'outer'))
- head_first_new: float32 [512, 400], P(('dp', 'outer'))
- head_second_new: float32 [512, 400], P(('dp', 'outer'))
- small_new: float32 [3728], replicated
- small_first_new: float32 [3728], replicated
- small_second_new: float32 [3728], replicated
- entry_copy: bfloat16 [256, 512], P(None, ('dp', 'outer'))
- spatial_copy: bfloat16 [9, 512, 1152], P(None, ('dp', 'outer'))
- temporal_copy: bfloat16 [3, 1152, 512], P(None, None, ('dp', 'outer'))
- head_copy: bfloat16 [512, 400], P(('dp', 'outer'))
Inputs may be any that keep to these rules, and one draw needn't show every extreme that they name: `valid_mask`: the valid positions of a clip form a box: its first k frames with k at least half of 4, and a centered block of rows and columns, at least half of 8 and of 8 long. `clip_keep`: the first clip is kept.
All inputs are finite; a program needn't handle non-finite values.
Results may differ from a plain program's by a relative error of at most 0.025.
The roundings to bfloat16 on the way count: a program that leaves them out, or rounds other values in their place, can miss the bound.
Values may be sent and summed in bfloat16 or wider, within the bound.
No kernel may reach another device: no remote copies, remote signals or barrier semaphores. Data moves between devices by JAX's collectives and lax.ppermute only.
A program may use at most 256 MiB of HBM per device.

v0:
```python
import jax
import jax.numpy as jnp
from jax import lax
from jax.sharding import PartitionSpec as P

CHANNELS = 512
HIDDEN_SIZE = 1152
CLASSES = 400


EPSILON = 1e-05
ADAM_EPS = 1e-08
DECAY_RATE = 0.1
SMOOTHING = 0.1


def contract_last(operand, factor):
    return lax.dot_general(
        operand, factor, (((1,), (1,)), ((), ())), preferred_element_type=jnp.float32
    )


def contract_first(operand, factor):
    return lax.dot_general(
        operand, factor, (((0,), (0,)), ((), ())), preferred_element_type=jnp.float32
    )


def spatial_columns(field):
    height, breadth = (field.shape[2], field.shape[3])
    padded = jnp.pad(field, ((0, 0), (0, 0), (1, 1), (1, 1), (0, 0)))
    pieces = [
        padded[:, :, offset // 3 : offset // 3 + height, offset % 3 : offset % 3 + breadth, :]
        for offset in range(9)
    ]
    return jnp.concatenate(pieces, axis=-1).reshape(-1, 9 * field.shape[4])


def spatial_back(columns, field_shape):
    height, breadth = (field_shape[2], field_shape[3])
    lattice = columns.reshape(field_shape[:4] + (9, field_shape[4]))
    padded = jnp.pad(lattice, ((0, 0), (0, 0), (1, 1), (1, 1), (0, 0), (0, 0)))
    summed = jnp.zeros(field_shape, jnp.float32)
    for offset in range(9):
        row_at = 2 - offset // 3
        col_at = 2 - offset % 3
        summed = (
            summed + padded[:, :, row_at : row_at + height, col_at : col_at + breadth, offset, :]
        )
    return summed


def temporal_columns(field):
    frames = field.shape[1]
    padded = jnp.pad(field, ((0, 0), (1, 1), (0, 0), (0, 0), (0, 0)))
    pieces = [padded[:, offset : offset + frames] for offset in range(3)]
    return jnp.concatenate(pieces, axis=-1).reshape(-1, 3 * field.shape[4])


def temporal_back(columns, field_shape):
    frames = field_shape[1]
    lattice = columns.reshape(field_shape[:4] + (3, field_shape[4]))
    padded = jnp.pad(lattice, ((0, 0), (1, 1), (0, 0), (0, 0), (0, 0), (0, 0)))
    summed = jnp.zeros(field_shape, jnp.float32)
    for offset in range(3):
        summed = summed + padded[:, 2 - offset : 2 - offset + frames, :, :, offset, :]
    return summed


def normalize(value, totals, squares, count, gain, shift):
    mean_val = totals / count
    variance = squares / count - mean_val * mean_val
    inverse = lax.rsqrt(variance + EPSILON)
    normed = (value - mean_val) * inverse
    return (normed, inverse, gain * normed + shift)


def norm_back(d_normed, normed, inverse, valid, sum_one, sum_two, count):
    return valid * inverse * (d_normed - sum_one / count - normed * (sum_two / count))


def adamw(master, grad, first, second, rate, decay, correction):
    first_new = 0.5 * first + 0.5 * grad
    second_new = 0.5 * second + 0.5 * grad * grad
    master_new = master - rate * (
        first_new / correction / (jnp.sqrt(second_new / correction) + ADAM_EPS) + decay * master
    )
    return (master_new, first_new, second_new)


def on_device(
    clip_frames,
    valid_mask,
    labels,
    clip_keep,
    step_count,
    w_entry,
    w_spatial,
    w_temporal,
    w_head,
    small_params,
    entry_first,
    entry_second,
    spatial_first,
    spatial_second,
    temporal_first,
    temporal_second,
    head_first,
    head_second,
    small_first,
    small_second,
):
    clip_local, frames, height, breadth, chan_local = clip_frames.shape
    row_total = clip_local * frames * height * breadth
    entry_low, spatial_low, temporal_low, head_low = (
        lax.all_gather(w_entry.astype(jnp.bfloat16), ("dp", "outer"), axis=1, tiled=True),
        lax.all_gather(w_spatial.astype(jnp.bfloat16), ("dp", "outer"), axis=1, tiled=True),
        lax.all_gather(w_temporal.astype(jnp.bfloat16), ("dp", "outer"), axis=2, tiled=True),
        lax.all_gather(w_head.astype(jnp.bfloat16), ("dp", "outer"), axis=0, tiled=True),
    )
    gain_one = small_params[:HIDDEN_SIZE]
    shift_one = small_params[HIDDEN_SIZE : 2 * HIDDEN_SIZE]
    gain_two = small_params[2 * HIDDEN_SIZE : 2 * HIDDEN_SIZE + CHANNELS]
    shift_two = small_params[2 * HIDDEN_SIZE + CHANNELS : 2 * HIDDEN_SIZE + 2 * CHANNELS]
    bias_vec = small_params[2 * HIDDEN_SIZE + 2 * CHANNELS :]
    valid = valid_mask.astype(jnp.float32).reshape(row_total, 1)
    inputs_flat = clip_frames.reshape(row_total, chan_local)
    field = jnp.dot(inputs_flat, entry_low, preferred_element_type=jnp.float32) * valid
    space_cols = spatial_columns(
        field.astype(jnp.bfloat16).reshape(clip_local, frames, height, breadth, CHANNELS)
    )
    conv_one = jnp.dot(
        space_cols,
        spatial_low.reshape(9 * CHANNELS, HIDDEN_SIZE),
        preferred_element_type=jnp.float32,
    )
    keep_float = clip_keep.astype(jnp.float32)
    count, kept, sum_one, square_one = lax.psum(
        (
            jnp.sum(valid),
            jnp.sum(keep_float),
            jnp.sum(conv_one * valid, axis=0),
            jnp.sum(conv_one * conv_one * valid, axis=0),
        ),
        ("dp", "outer"),
    )
    normed_one, inverse_one, pre_one = normalize(
        conv_one, sum_one, square_one, count, gain_one, shift_one
    )
    first = jnp.maximum(pre_one, 0.0) * valid
    time_cols = temporal_columns(
        first.astype(jnp.bfloat16).reshape(clip_local, frames, height, breadth, HIDDEN_SIZE)
    )
    conv_two = jnp.dot(
        time_cols,
        temporal_low.reshape(3 * HIDDEN_SIZE, CHANNELS),
        preferred_element_type=jnp.float32,
    )
    sum_two, square_two = lax.psum(
        (jnp.sum(conv_two * valid, axis=0), jnp.sum(conv_two * conv_two * valid, axis=0)),
        ("dp", "outer"),
    )
    normed_two, inverse_two, affine_two = normalize(
        conv_two, sum_two, square_two, count, gain_two, shift_two
    )
    pre_two = affine_two + field
    second = jnp.maximum(pre_two, 0.0) * valid
    clip_count = jnp.sum(valid.reshape(clip_local, -1), axis=1)[:, None]
    pooled = jnp.sum(second.reshape(clip_local, -1, CHANNELS), axis=1) / clip_count
    pooled_low = pooled.astype(jnp.bfloat16)
    logits = jnp.dot(pooled_low, head_low, preferred_element_type=jnp.float32) + bias_vec
    log_prob = jax.nn.log_softmax(logits, axis=-1)
    target = (1.0 - SMOOTHING) * (labels[:, None] == jnp.arange(CLASSES)[None, :]).astype(
        jnp.float32
    ) + SMOOTHING / CLASSES
    local_loss = jnp.sum(keep_float * -jnp.sum(target * log_prob, axis=-1))
    d_logits = keep_float[:, None] * (jnp.exp(log_prob) - target) / kept
    d_low = d_logits.astype(jnp.bfloat16)
    grad_head = contract_first(pooled_low, d_low)
    d_pooled = contract_last(d_low, head_low) / clip_count
    d_second = jnp.broadcast_to(
        d_pooled[:, None, :], (clip_local, frames * height * breadth, CHANNELS)
    ).reshape(row_total, CHANNELS)
    d_pre_two = d_second * valid * (pre_two > 0.0).astype(jnp.float32)
    d_normed_two = d_pre_two * gain_two
    back_one, back_two, loss_sum = lax.psum(
        (jnp.sum(d_normed_two, axis=0), jnp.sum(d_normed_two * normed_two, axis=0), local_loss),
        ("dp", "outer"),
    )
    d_conv_two = norm_back(
        d_normed_two, normed_two, inverse_two, valid, back_one, back_two, count
    ).astype(jnp.bfloat16)
    grad_temporal = contract_first(time_cols, d_conv_two).reshape(3, HIDDEN_SIZE, CHANNELS)
    d_first = temporal_back(
        contract_last(d_conv_two, temporal_low.reshape(3 * HIDDEN_SIZE, CHANNELS)),
        (clip_local, frames, height, breadth, HIDDEN_SIZE),
    ).reshape(row_total, HIDDEN_SIZE)
    d_pre_one = d_first * valid * (pre_one > 0.0).astype(jnp.float32)
    d_normed_one = d_pre_one * gain_one
    small_local = jnp.concatenate(
        [
            jnp.sum(d_pre_one * normed_one, axis=0),
            jnp.sum(d_pre_one, axis=0),
            jnp.sum(d_pre_two * normed_two, axis=0),
            jnp.sum(d_pre_two, axis=0),
            jnp.sum(d_logits, axis=0),
        ]
    )
    back_three, back_four, small_grad = lax.psum(
        (jnp.sum(d_normed_one, axis=0), jnp.sum(d_normed_one * normed_one, axis=0), small_local),
        ("dp", "outer"),
    )
    d_conv_one = norm_back(
        d_normed_one, normed_one, inverse_one, valid, back_three, back_four, count
    ).astype(jnp.bfloat16)
    grad_spatial = contract_first(space_cols, d_conv_one).reshape(9, CHANNELS, HIDDEN_SIZE)
    d_field = (
        spatial_back(
            contract_last(d_conv_one, spatial_low.reshape(9 * CHANNELS, HIDDEN_SIZE)),
            (clip_local, frames, height, breadth, CHANNELS),
        ).reshape(row_total, CHANNELS)
        + d_pre_two
    )
    d_entry = (d_field * valid).astype(jnp.bfloat16)
    grad_entry = contract_first(inputs_flat, d_entry)
    entry_share, spatial_share, temporal_share, head_share = (
        lax.psum_scatter(grad_entry, ("dp", "outer"), scatter_dimension=1, tiled=True),
        lax.psum_scatter(grad_spatial, ("dp", "outer"), scatter_dimension=1, tiled=True),
        lax.psum_scatter(grad_temporal, ("dp", "outer"), scatter_dimension=2, tiled=True),
        lax.psum_scatter(grad_head, ("dp", "outer"), scatter_dimension=0, tiled=True),
    )
    correction = 1.0 - jnp.power(0.5, step_count[0].astype(jnp.float32))
    entry_out = adamw(w_entry, entry_share, entry_first, entry_second, 0.06, DECAY_RATE, correction)
    spatial_out = adamw(
        w_spatial, spatial_share, spatial_first, spatial_second, 0.02, DECAY_RATE, correction
    )
    temporal_out = adamw(
        w_temporal, temporal_share, temporal_first, temporal_second, 0.02, DECAY_RATE, correction
    )
    head_out = adamw(w_head, head_share, head_first, head_second, 0.05, DECAY_RATE, correction)
    small_out = adamw(small_params, small_grad, small_first, small_second, 0.5, 0.0, correction)
    return (
        loss_sum / kept,
        entry_out[0],
        entry_out[1],
        entry_out[2],
        spatial_out[0],
        spatial_out[1],
        spatial_out[2],
        temporal_out[0],
        temporal_out[1],
        temporal_out[2],
        head_out[0],
        head_out[1],
        head_out[2],
        small_out[0],
        small_out[1],
        small_out[2],
        entry_out[0].astype(jnp.bfloat16),
        spatial_out[0].astype(jnp.bfloat16),
        temporal_out[0].astype(jnp.bfloat16),
        head_out[0].astype(jnp.bfloat16),
    )


def solution(mesh):
    placed = (
        P(("dp", "outer"), None, None, None, None),
        P(("dp", "outer"), None, None, None),
        P(("dp", "outer")),
        P(("dp", "outer")),
        P(),
        P(None, ("dp", "outer")),
        P(None, ("dp", "outer"), None),
        P(None, None, ("dp", "outer")),
        P(("dp", "outer"), None),
        P(),
        P(None, ("dp", "outer")),
        P(None, ("dp", "outer")),
        P(None, ("dp", "outer"), None),
        P(None, ("dp", "outer"), None),
        P(None, None, ("dp", "outer")),
        P(None, None, ("dp", "outer")),
        P(("dp", "outer"), None),
        P(("dp", "outer"), None),
        P(),
        P(),
    )
    return jax.shard_map(
        on_device,
        mesh=mesh,
        in_specs=placed,
        out_specs=(
            P(),
            P(None, ("dp", "outer")),
            P(None, ("dp", "outer")),
            P(None, ("dp", "outer")),
            P(None, ("dp", "outer"), None),
            P(None, ("dp", "outer"), None),
            P(None, ("dp", "outer"), None),
            P(None, None, ("dp", "outer")),
            P(None, None, ("dp", "outer")),
            P(None, None, ("dp", "outer")),
            P(("dp", "outer"), None),
            P(("dp", "outer"), None),
            P(("dp", "outer"), None),
            P(),
            P(),
            P(),
            P(None, ("dp", "outer")),
            P(None, ("dp", "outer"), None),
            P(None, None, ("dp", "outer")),
            P(("dp", "outer"), None),
        ),
        check_vma=False,
    )
```

profile of v0, /device:TPU:0, one launch (start us, length us, event | category | flops | bytes accessed | tf_op | source)
XLA Modules:
  0.0 1130.6 jit_solution(17860277700115364943)
XLA Ops:
  17.7 71.8 %all_gather.12 = bf16[256,512]{0,1:T(8,128)(2,1)S(1)} all-gather(bf16[256,16]{0,1:T(8,128)(2,1)S(1)} %convert_element_type.67), channel_id=1, replica_groups=mesh['dp'=16,'outer'=2] {'dp','outer'}, dimensions={1}, use_global_device_ids=true | all-gather | bytes 270336 | tf_op jit(solution)/shard_map/all_gather | solution.py:116
  89.5 69.2 %all_gather.15 = bf16[512,400]{1,0:T(8,128)(2,1)S(1)} all-gather(bf16[16,400]{1,0:T(8,128)(2,1)S(1)} %convert_element_type.74), channel_id=1, replica_groups=mesh['dp'=16,'outer'=2] {'dp','outer'}, dimensions={0}, use_global_device_ids=true | all-gather | bytes 422400 | tf_op jit(solution)/shard_map/all_gather | solution.py:119
  180.0 5.8 copy.43
  185.8 32.0 %multiply_reduce_fusion.3 = (f32[1152]{0:T(1024)S(1)}, f32[1152]{0:T(1024)S(1)}, f32[2048,1152]{1,0:T(8,128)}) fusion(f32[2048]{0:T(1024)S(1)} %mul.326, bf16[2048,4608]{1,0:T(8,128)(2,1)} %constant_dynamic-update-slice_fusion, bf16[4608,1152]{1,0:T(8,128)(2,1)} %bitcast.137), kind=kOutput, calls=%fused_computation.32 | convolution fusion | flops 21755064320 | bytes 38945792 | tf_op jit(solution)/shard_map/dot_general | solution.py:132
  217.8 37.8 %all-reduce.7 = (f32[1152]{0:T(1024)S(1)}, f32[]{:T(128)}, f32[1152]{0:T(1024)S(1)}) all-reduce(f32[1152]{0:T(1024)S(1)} %get-tuple-element.25, f32[]{:T(128)} %get-tuple-element.33, f32[1152]{0:T(1024)S(1)} %get-tuple-element.24), channel_id=1, replica_groups=mesh['dp'=16,'outer'=2] {'dp','outer'}, use_global_device_ids=true, to_apply=%region_5.6 | all-reduce | flops 2305 | bytes 18440 | tf_op jit(solution)/shard_map/psum | solution.py:138
  264.9 12.9 %multiply_reduce_fusion.6 = (f32[512]{0:T(512)S(1)}, f32[512]{0:T(512)S(1)}, f32[2048,512]{1,0:T(8,128)}) fusion(f32[2048]{0:T(1024)S(1)} %mul.326, bf16[3456,512]{1,0:T(8,128)(2,1)} %bitcast.135, bf16[2048,1152]{1,0:T(8,128)(2,1)} %bitcast.121, bf16[2048,1152]{1,0:T(8,128)(2,1)S(1)} %multiply_convert_fusion.1, bf16[2048,1152]{1,0:T(8,128)(2,1)S(1)} %bitcast.119), kind=kOutput, calls=%fused_computation.69 | convolution fusion | flops 7295466496 | bytes 21901312 | tf_op jit(solution)/shard_map/dot_general | solution.py:154
  277.8 42.9 %all-reduce.6 = (f32[]{:T(128)}, f32[512]{0:T(512)S(1)}, f32[512]{0:T(512)S(1)}) all-reduce(f32[]{:T(128)} %convert_reduce_fusion.2, f32[512]{0:T(512)S(1)} %get-tuple-element.29, f32[512]{0:T(512)S(1)} %get-tuple-element.28), channel_id=1, replica_groups=mesh['dp'=16,'outer'=2] {'dp','outer'}, use_global_device_ids=true, to_apply=%region_18.19 | all-reduce | flops 1025 | bytes 8200 | tf_op jit(solution)/shard_map/psum | solution.py:138
  331.7 38.5 %all-reduce.5 = (f32[512]{0:T(512)S(1)}, f32[512]{0:T(512)S(1)}) all-reduce(f32[512]{0:T(512)S(1)} %get-tuple-element.27, f32[512]{0:T(512)S(1)} %get-tuple-element.30), channel_id=1, replica_groups=mesh['dp'=16,'outer'=2] {'dp','outer'}, use_global_device_ids=true, to_apply=%region_22.23 | all-reduce | flops 1024 | bytes 8192 | tf_op jit(solution)/shard_map/psum | solution.py:186
  375.3 13.3 %fusion.31 = f32[8,4,8,8,3,1152]{5,3,4,2,1,0:T(8,128)} fusion(bf16[8,4,8,8,512,1]{4,3,5,2,1,0:T(8,128)(2,1)S(1)} %bitcast.136, bf16[3,1152,512]{1,2,0:T(8,128)(2,1)S(1)} %copy-done.8), kind=kOutput, calls=%fused_computation.71 | convolution fusion | flops 7247757312 | bytes 33947648 | tf_op jit(solution)/shard_map/dot_general | solution.py:18
  388.6 9.0 fusion.3
  397.7 5.5 fusion.45
  403.3 43.0 %all-reduce.4 = (f32[]{:T(128)}, f32[1152]{0:T(1024)S(1)}, f32[1152]{0:T(1024)S(1)}, f32[3728]{0:T(1024)}) all-reduce(f32[]{:T(128)} %multiply_reduce_fusion.8, f32[1152]{0:T(1024)S(1)} %get-tuple-element.22, f32[1152]{0:T(1024)S(1)} %get-tuple-element.23, ...), channel_id=1, replica_groups=mesh['dp'=16,'outer'=2] {'dp','outer'}, use_global_device_ids=true, to_apply=%region_16.17 | all-reduce | flops 6033 | bytes 48264 | tf_op jit(solution)/shard_map/psum | solution.py:186
  447.0 11.3 multiply_convert_fusion
  458.2 33.1 %fusion = f32[8,4,8,8,9,512]{5,3,4,2,1,0:T(8,128)} fusion(bf16[8,4,8,8,1152,1]{4,3,5,2,1,0:T(8,128)(2,1)} %bitcast.134, bf16[9,512,1152]{2,1,0:T(8,128)(2,1)} %all-gather.3.cloned.1.call-done), kind=kOutput, calls=%fused_computation.19 | convolution fusion | flops 21743271936 | bytes 53084160 | tf_op jit(solution)/shard_map/dot_general | solution.py:18
  491.3 13.5 %fusion.15 = f32[8,4,8,8,1,512]{5,3,4,2,1,0:T(8,128)S(1)} fusion(f32[8,4,8,8,9,512]{5,3,4,2,1,0:T(8,128)} %fusion), kind=kLoop, calls=%fused_computation.46 | loop fusion | flops 8388608 | bytes 46137344 | tf_op jit(solution)/shard_map/add | solution.py:48
  509.7 12.7 %fusion.5 = bf16[3456,2048]{0,1:T(8,128)(2,1)} fusion(bf16[2048,1152]{1,0:T(8,128)(2,1)} %bitcast.122, bf16[2048,1152]{1,0:T(8,128)(2,1)} %copy-done.2, bf16[2048,1152]{1,0:T(8,128)(2,1)} %bitcast.120), kind=kLoop, calls=%fused_computation.36 | loop fusion | flops 42467328 | bytes 28311552 | tf_op jit(solution)/shard_map/dot_general | solution.py:24
  522.4 18.8 %copy.45 = bf16[3456,2048]{1,0:T(8,128)(2,1)} copy(bf16[3456,2048]{0,1:T(8,128)(2,1)} %fusion.5) | data formatting | bytes 28311552 | tf_op jit(solution)/shard_map/dot_general | solution.py:24
  541.2 12.8 %fusion.33 = f32[3,1152,512]{1,2,0:T(8,128)} fusion(bf16[3,1152,2048]{2,1,0:T(8,128)(2,1)} %bitcast.125, bf16[2048,512]{1,0:T(8,128)(2,1)S(1)} %copy-done.11), kind=kOutput, calls=%fused_computation.73 | convolution fusion | flops 7247757312 | bytes 23330816 | tf_op jit(solution)/shard_map/dot_general | solution.py:24
  554.1 23.2 %copy.44 = bf16[4608,2048]{1,0:T(8,128)(2,1)} copy(bf16[4608,2048]{0,1:T(8,128)(2,1)} %bitcast.31) | data formatting | bytes 37748736 | tf_op jit(solution)/shard_map/dot_general | solution.py:24
  577.4 31.4 %fusion.7 = f32[9,512,1152]{2,1,0:T(8,128)} fusion(bf16[9,512,2048]{2,1,0:T(8,128)(2,1)} %bitcast.124, bf16[2048,1152]{1,0:T(8,128)(2,1)} %multiply_convert_fusion), kind=kOutput, calls=%fused_computation.38 | convolution fusion | flops 21743271936 | bytes 44826624 | tf_op jit(solution)/shard_map/dot_general | solution.py:24
  612.5 28.7 %reduce-scatter.5.cloned.1.call-done = f32[256,16]{0,1:T(8,128)} async-done(((f32[256,512]{0,1:T(8,128)}), f32[256,16]{0,1:T(8,128)}) %reduce-scatter.5.cloned.1.call-update) | async-done | bytes 16400 | tf_op jit(solution)/shard_map/reduce_scatter | solution.py:227
  642.5 131.5 %reduce-scatter.11.cloned.1.call-done = f32[16,400]{1,0:T(8,128)} async-done(((f32[512,400]{1,0:T(8,128)}), f32[16,400]{1,0:T(8,128)}) %reduce-scatter.11.cloned.1.call-update) | async-done | bytes 25616 | tf_op jit(solution)/shard_map/reduce_scatter | solution.py:230
  775.5 119.4 %reduce-scatter.9.cloned.1.call-done = f32[3,1152,16]{1,2,0:T(8,128)} async-done(((f32[3,1152,512]{1,2,0:T(8,128)}), f32[3,1152,16]{1,2,0:T(8,128)}) %reduce-scatter.9.cloned.1.call-update) | async-done | bytes 221200 | tf_op jit(solution)/shard_map/reduce_scatter | solution.py:229
  896.9 222.7 %reduce-scatter.7.cloned.1.call-done = f32[9,16,1152]{2,1,0:T(8,128)} async-done(((f32[9,512,1152]{2,1,0:T(8,128)}), f32[9,16,1152]{2,1,0:T(8,128)}) %reduce-scatter.7.cloned.1.call-update) | async-done | bytes 663568 | tf_op jit(solution)/shard_map/reduce_scatter | solution.py:228
  (150 shorter events, 71.5 us)
Async XLA Ops:
  7.2 153.0 %copy-start = (bf16[8,4,8,8,256]{4,3,2,1,0:T(8,128)(2,1)S(1)}, bf16[8,4,8,8,256]{4,3,2,1,0:T(8,128)(2,1)}, u32[]{:S(2)}) copy-start(bf16[8,4,8,8,256]{4,3,2,1,0:T(8,128)(2,1)} %param.20) | copy-start | bytes 3145732
  7.2 172.8 %all-gather.5.cloned.1.call-start = ((), (), s32[]{:S(2)}) async-start(), calls=%async_computation.5 | async-start | bytes 3649536 | tf_op jit(solution)/shard_map/all_gather | solution.py:118
  8.9 176.9 %all-gather.3.cloned.1.call-start = ((), (), s32[]{:S(2)}) async-start(), calls=%async_computation.4 | async-start | bytes 10948608 | tf_op jit(solution)/shard_map/all_gather | solution.py:117
  10.9 630.2 %reduce-scatter.5.cloned.1.call-start = ((), (), s32[]{:S(2)}) async-start(), calls=%async_computation.6 | async-start | bytes 540672 | tf_op jit(solution)/shard_map/reduce_scatter | solution.py:227
  11.6 315.7 %copy-start.33 = (f32[8]{0:T(128)}, f32[8]{0:T(128)S(1)}, u32[]{:S(2)}) copy-start(f32[8]{0:T(128)S(1)} %convert_element_type.66) | copy-start | bytes 100
  14.8 432.2 %copy-start.15 = (f32[2048]{0:T(1024)}, f32[2048]{0:T(1024)S(1)}, u32[]{:S(2)}) copy-start(f32[2048]{0:T(1024)S(1)} %mul.326) | copy-start | bytes 24580
  17.7 308.6 %copy-start.29 = (f32[8]{0:T(128)}, f32[8]{0:T(128)S(1)}, u32[]{:S(2)}) copy-start(f32[8]{0:T(128)S(1)} %get-tuple-element.32) | copy-start | bytes 100
  277.8 48.5 %copy-start.31 = (s32[8]{0:T(128)S(1)}, s32[8]{0:T(128)}, u32[]{:S(2)}) copy-start(s32[8]{0:T(128)} %param.22) | copy-start | bytes 100
  327.3 44.6 %copy-start.20 = (f32[8,512]{1,0:T(8,128)}, f32[8,512]{1,0:T(8,128)S(1)}, u32[]{:S(2)}) copy-start(f32[8,512]{1,0:T(8,128)S(1)} %convolution_divide_fusion) | copy-start | bytes 49156
  331.0 57.7 %copy-start.6 = (pred[2048,512]{1,0:T(8,128)(4,1)}, pred[2048,512]{1,0:T(8,128)(4,1)S(1)}, u32[]{:S(2)}) copy-start(pred[2048,512]{1,0:T(8,128)(4,1)S(1)} %get-tuple-element.67) | copy-start | bytes 3145732
  375.3 22.4 %slice-start = ((s8[9437184]{0:T(1024)(128)(4,1)}), s8[4194304]{0:T(1024)(128)(4,1)S(1)}, s32[]{:S(2)}) async-start(s8[9437184]{0:T(1024)(128)(4,1)} %bitcast.116), calls=%async_computation.10 | async-start | bytes 8388608
  375.3 22.4 %slice-start.1 = ((s8[9437184]{0:T(1024)(128)(4,1)}), s8[1048576]{0:T(1024)(128)(4,1)S(1)}, s32[]{:S(2)}) async-start(s8[9437184]{0:T(1024)(128)(4,1)} %bitcast.116), calls=%async_computation.11 | async-start | bytes 2097152
  491.3 13.6 %copy-start.21 = (f32[8,512]{1,0:T(8,128)S(1)}, f32[8,512]{1,0:T(8,128)}, u32[]{:S(2)}) copy-start(f32[8,512]{1,0:T(8,128)} %copy-done.20) | copy-start | bytes 49156
  507.5 266.6 %reduce-scatter.11.cloned.1.call-start = ((), (), s32[]{:S(2)}) async-start(), calls=%async_computation.9 | async-start | bytes 1081344 | tf_op jit(solution)/shard_map/reduce_scatter | solution.py:230
  509.7 385.2 %reduce-scatter.9.cloned.1.call-start = ((), (), s32[]{:S(2)}) async-start(), calls=%async_computation.8 | async-start | bytes 7299072 | tf_op jit(solution)/shard_map/reduce_scatter | solution.py:229
  522.4 18.8 %copy-start.11 = (bf16[2048,512]{1,0:T(8,128)(2,1)S(1)}, bf16[2048,512]{1,0:T(8,128)(2,1)}, u32[]{:S(2)}) copy-start(bf16[2048,512]{1,0:T(8,128)(2,1)} %copy-done.10) | copy-start | bytes 6291460
  554.1 565.5 %reduce-scatter.7.cloned.1.call-start = ((), (), s32[]{:S(2)}) async-start(), calls=%async_computation.7 | async-start | bytes 21897216 | tf_op jit(solution)/shard_map/reduce_scatter | solution.py:228
  608.8 32.3 %copy-start.26 = (f32[256,16]{0,1:T(8,128)S(1)}, f32[256,16]{0,1:T(8,128)}, u32[]{:S(2)}) copy-start(f32[256,16]{0,1:T(8,128)} %param.25) | copy-start | bytes 49156
  608.8 165.2 %copy-start.24 = (f32[16,400]{1,0:T(8,128)S(1)}, f32[16,400]{1,0:T(8,128)}, u32[]{:S(2)}) copy-start(f32[16,400]{1,0:T(8,128)} %param.28) | copy-start | bytes 76804
  608.8 286.1 %copy-start.12 = (f32[3,1152,16]{1,2,0:T(8,128)S(1)}, f32[3,1152,16]{1,2,0:T(8,128)}, u32[]{:S(2)}) copy-start(f32[3,1152,16]{1,2,0:T(8,128)} %param.27) | copy-start | bytes 663556
  608.8 286.0 %copy-start.19 = (f32[3,1152,16]{1,2,0:T(8,128)S(1)}, f32[3,1152,16]{1,2,0:T(8,128)}, u32[]{:S(2)}) copy-start(f32[3,1152,16]{1,2,0:T(8,128)} %param.35) | copy-start | bytes 663556
  608.8 510.8 %copy-start.9 = (f32[9,16,1152]{2,1,0:T(8,128)S(1)}, f32[9,16,1152]{2,1,0:T(8,128)}, u32[]{:S(2)}) copy-start(f32[9,16,1152]{2,1,0:T(8,128)} %param.26) | copy-start | bytes 1990660
  608.8 510.8 %copy-start.13 = (f32[9,16,1152]{2,1,0:T(8,128)S(1)}, f32[9,16,1152]{2,1,0:T(8,128)}, u32[]{:S(2)}) copy-start(f32[9,16,1152]{2,1,0:T(8,128)} %param.33) | copy-start | bytes 1990660
  608.9 510.8 %copy-start.14 = (f32[9,16,1152]{2,1,0:T(8,128)S(1)}, f32[9,16,1152]{2,1,0:T(8,128)}, u32[]{:S(2)}) copy-start(f32[9,16,1152]{2,1,0:T(8,128)} %param.32) | copy-start | bytes 1990660
  (23 other events, 130.3 us)
Sparse Core Ops, SparseCore 0:
  11.6 63.6 all-gather.4
  78.8 87.9 all-gather.2
  507.6 133.4 reduce-scatter.4
  643.3 130.6 reduce-scatter.10
  779.6 115.2 reduce-scatter.8
  902.3 217.2 reduce-scatter.6
where the time goes:
time: 1140 us; the launch traced here: 1130 us
  waiting for transfers between devices  502 us (44%)
  blocking collectives  303 us (27%)
  matrix products  143 us (13%)
  other arithmetic  92 us (8%)
  local copies, waits for them, and re-layouts  71.4 us (6%)
  between operations  18.3 us (2%)
    reduce_scatter x1, waiting for transfers between devices, on_device(): lax.psum_scatter(grad_spatial, ('dp', 'outer'), scatter_dimension=1, tile...  223 us
    reduce_scatter x1, waiting for transfers between devices, on_device(): lax.psum_scatter(grad_head, ('dp', 'outer'), scatter_dimension=0, tiled=T...  132 us
    reduce_scatter x1, waiting for transfers between devices, on_device(): lax.psum_scatter(grad_temporal, ('dp', 'outer'), scatter_dimension=2, til...  119 us
    psum x2, blocking collectives, on_device(): lax.psum((jnp.sum(d_normed_two, axis=0), jnp.sum(d_normed_two * normed_tw...  81.5 us
    psum x2, blocking collectives, on_device(): lax.psum((jnp.sum(valid), jnp.sum(keep_float), jnp.sum(conv_one * valid,...  80.8 us
    all_gather x1, blocking collectives, on_device(): lax.all_gather(w_entry.astype(jnp.bfloat16), ('dp', 'outer'), axis=1, til...  71.8 us
    all_gather x1, blocking collectives, on_device(): lax.all_gather(w_head.astype(jnp.bfloat16), ('dp', 'outer'), axis=0, tile...  69.2 us
    dot_general x4, matrix products, contract_first(): lax.dot_general(operand, factor, (((0,), (0,)), ((), ())), preferred_elem...  47.8 us
  transfers between devices with their start and end apart: 6, of which 4 were waited for; matrix products, arithmetic and copies ran while one was open for 13% of the time, Pallas kernels for 0%

commit v1 on v0

v1 whole, which is shorter than its diff:
```python
import functools

import jax
import jax.numpy as jnp
from jax import lax
from jax.experimental import pallas as pl
from jax.experimental.pallas import tpu as pltpu
from jax.sharding import PartitionSpec as P

CHANNELS = 512
HIDDEN = 1152
CLASSES = 400
CHAN_IN = 256

EPSILON = 1e-05
ADAM_EPS = 1e-08
DECAY_RATE = 0.1
SMOOTHING = 0.1

AXES = ("dp", "outer")
BF = jnp.bfloat16
F32 = jnp.float32
MIB = 1 << 20
EXACT = lax.Precision.HIGHEST


def wide(column, times):
    return jnp.concatenate([column] * times, axis=1)


def dot_nn(left, right):
    return lax.dot_general(left, right, (((1,), (0,)), ((), ())), preferred_element_type=F32)


def dot_nt(left, right):
    return lax.dot_general(left, right, (((1,), (1,)), ((), ())), preferred_element_type=F32)


def dot_tn(left, right):
    return lax.dot_general(left, right, (((0,), (0,)), ((), ())), preferred_element_type=F32)


def to_owner_order(row, order):
    return lax.dot_general(
        row, order, (((1,), (0,)), ((), ())), precision=EXACT, preferred_element_type=F32
    )


def to_local_order(row, order):
    return lax.dot_general(
        row, order, (((1,), (1,)), ((), ())), precision=EXACT, preferred_element_type=F32
    )


def fold(value, step):
    return jnp.sum(value.reshape(value.shape[0] // step, step, value.shape[1]), axis=0)


def whole(shape):
    return pl.BlockSpec(shape, lambda *_: (0,) * len(shape))


def call(kernel, name, grid, in_specs, out_specs, out_shape, scratch=(), aliases=None, vmem=40, flops=0):
    return pl.pallas_call(
        kernel,
        name=name,
        grid=grid,
        in_specs=in_specs,
        out_specs=out_specs,
        out_shape=out_shape,
        scratch_shapes=list(scratch),
        input_output_aliases=aliases or {},
        compiler_params=pltpu.CompilerParams(vmem_limit_bytes=vmem * MIB),
        cost_estimate=pl.CostEstimate(flops=flops, bytes_accessed=20 * MIB, transcendentals=0),
    )


def entry_kernel(count, side, clips, x_ref, valid_ref, *refs):
    pieces, (field_ref, cols_ref, conv_ref, w_ref, e_ref) = refs[:count], refs[count:]

    @pl.when(pl.program_id(0) == 0)
    def _():
        at = 0
        for piece in pieces:
            rows = piece.shape[0]
            for b in range(3):
                w_ref[b * CHANNELS + at : b * CHANNELS + at + rows, :] = piece[
                    :, b * HIDDEN : (b + 1) * HIDDEN
                ]
            e_ref[at : at + rows, :] = piece[:, 3 * HIDDEN :]
            at += rows

    value = dot_nt(x_ref[...], e_ref[...]) * wide(valid_ref[...], CHANNELS // 128)
    field_ref[...] = value
    rows = value.shape[0]
    group = side * clips
    grid3 = value.reshape(rows // group, group, CHANNELS)
    edge = jnp.zeros((rows // group, clips, CHANNELS), F32)
    left = jnp.concatenate([edge, grid3[:, : group - clips]], axis=1).reshape(rows, CHANNELS)
    right = jnp.concatenate([grid3[:, clips:], edge], axis=1).reshape(rows, CHANNELS)
    cols_ref[:, :CHANNELS] = left.astype(BF)
    cols_ref[:, CHANNELS : 2 * CHANNELS] = value.astype(BF)
    cols_ref[:, 2 * CHANNELS :] = right.astype(BF)
    conv_ref[...] = dot_nn(cols_ref[...], w_ref[...])


def spatial_kernel(count, tap_row, group, cols_ref, conv_ref, *refs):
    pieces, refs = refs[:count], refs[count:]
    step = pl.program_id(0)
    if tap_row == 0:
        out_ref, w_ref = refs
    else:
        valid_ref, keep_ref, out_ref, stats_ref, w_ref, acc_ref = refs

    @pl.when(step == 0)
    def _():
        at = 0
        for piece in pieces:
            rows = piece.shape[0]
            for b in range(3):
                w_ref[b * CHANNELS + at : b * CHANNELS + at + rows, :] = piece[
                    :, b * HIDDEN : (b + 1) * HIDDEN
                ]
            at += rows

    rows = cols_ref.shape[0]
    if tap_row == 0:
        out_ref[:group] = conv_ref[:group]
        out_ref[group:] = conv_ref[group:] + dot_nn(cols_ref[: rows - group], w_ref[...])
        return
    out_ref[rows - group :] = conv_ref[rows - group :]
    out_ref[: rows - group] = conv_ref[: rows - group] + dot_nn(cols_ref[group:], w_ref[...])

    @pl.when(step == 0)
    def _():
        acc_ref[...] = jnp.zeros_like(acc_ref)

    value = out_ref[...]
    kept = value * wide(valid_ref[...], HIDDEN // 128)
    acc_ref[:, :HIDDEN] += fold(kept, 8)
    acc_ref[:, HIDDEN : 2 * HIDDEN] += fold(kept * value, 8)
    acc_ref[:, 2 * HIDDEN : 2 * HIDDEN + 128] += fold(valid_ref[...], 8)

    @pl.when(step == pl.num_programs(0) - 1)
    def _():
        acc_ref[:, 2 * HIDDEN + 128 :] = fold(keep_ref[...], 8)
        stats_ref[...] = jnp.sum(acc_ref[...], axis=0, keepdims=True)


def temporal_kernel(
    count, frames, recv_ref, conv_ref, valid_ref, valid_out_ref, gain_ref, shift_ref, order_ref, *refs
):
    pieces, refs = refs[:count], refs[count:]
    first_ref, two_ref, stats_ref, coef_ref, head_ref, w_ref, first_all, acc_ref = refs
    step = pl.program_id(0)
    per = conv_ref.shape[0]

    @pl.when(step == 0)
    def _():
        at = 0
        for piece in pieces:
            rows = piece.shape[0]
            head_ref[at : at + rows, :] = piece[:, :CHANNELS]
            w_ref[at : at + rows, :] = piece[:, CHANNELS:]
            at += rows
        total = jnp.sum(recv_ref[...], axis=0)
        count_all = total[:, 2 * HIDDEN : 2 * HIDDEN + 128]
        wide_count = wide(count_all, HIDDEN // 128)
        mean = total[:, :HIDDEN] / wide_count
        variance = total[:, HIDDEN : 2 * HIDDEN] / wide_count - mean * mean
        coef_ref[...] = jnp.zeros_like(coef_ref)
        coef_ref[0:1, :HIDDEN] = mean
        coef_ref[1:2, :HIDDEN] = lax.rsqrt(variance + EPSILON)
        coef_ref[2:3, :HIDDEN] = gain_ref[...]
        coef_ref[3:4, :HIDDEN] = shift_ref[...]
        coef_ref[0:1, HIDDEN:] = count_all
        coef_ref[1:2, HIDDEN:] = total[:, 2 * HIDDEN + 128 :]
        acc_ref[...] = jnp.zeros_like(acc_ref)

    @pl.when(step < frames)
    def _():
        normed = (conv_ref[...] - coef_ref[0:1, :HIDDEN]) * coef_ref[1:2, :HIDDEN]
        pre = coef_ref[2:3, :HIDDEN] * normed + coef_ref[3:4, :HIDDEN]
        first = (jnp.maximum(pre, 0.0) * wide(valid_ref[...], HIDDEN // 128)).astype(BF)
        first_ref[...] = first
        first_all[pl.ds(pl.multiple_of(step * per, per), per), :] = first

    def frame(start, taps):
        pieces_at = [
            first_all[pl.ds(pl.multiple_of(start + k * per, per), per), :] for k in range(len(taps))
        ]
        lanes = slice(taps[0] * HIDDEN, (taps[-1] + 1) * HIDDEN)
        value = dot_nt(jnp.concatenate(pieces_at, axis=1), w_ref[:, lanes])
        two_ref[...] = value
        kept = value * wide(valid_out_ref[...], CHANNELS // 128)
        acc_ref[:, :CHANNELS] += fold(kept, 8)
        acc_ref[:, CHANNELS:] += fold(kept * value, 8)

    @pl.when(step == 1)
    def _():
        frame(0, (1, 2))

    @pl.when(jnp.logical_and(step > 1, step < frames))
    def _():
        frame((step - 2) * per, (0, 1, 2))

    @pl.when(step == frames)
    def _():
        frame((frames - 2) * per, (0, 1))
        sums = jnp.sum(acc_ref[...], axis=0, keepdims=True)
        stats_ref[:, :CHANNELS] = to_owner_order(sums[:, :CHANNELS], order_ref[...])
        stats_ref[:, CHANNELS:] = to_owner_order(sums[:, CHANNELS:], order_ref[...])


def head_kernel(
    clips, recv_ref, two_ref, field_ref, valid_ref, coef_ref, gain_ref, shift_ref, order_ref,
    head_ref, bias_ref, target_ref, keep_ref,
    dpool_ref, stats_ref, coef_two_ref, keep_grad_ref, send_grad_ref, acc_ref, size_ref,
):
    step = pl.program_id(0)

    @pl.when(step == 0)
    def _():
        total = jnp.sum(recv_ref[...], axis=0)
        count = wide(coef_ref[0:1, HIDDEN:], CHANNELS // 128)
        mean = to_local_order(total[:, :CHANNELS], order_ref[...]) / count
        square = to_local_order(total[:, CHANNELS:], order_ref[...]) / count
        coef_two_ref[...] = jnp.zeros_like(coef_two_ref)
        coef_two_ref[0:1, :] = mean
        coef_two_ref[1:2, :] = lax.rsqrt(square - mean * mean + EPSILON)
        coef_two_ref[2:3, :] = to_local_order(gain_ref[...], order_ref[...])
        coef_two_ref[3:4, :] = to_local_order(shift_ref[...], order_ref[...])
        acc_ref[...] = jnp.zeros_like(acc_ref)
        size_ref[...] = jnp.zeros_like(size_ref)

    valid = wide(valid_ref[...], CHANNELS // 128)
    normed = (two_ref[...] - coef_two_ref[0:1, :]) * coef_two_ref[1:2, :]
    pre = coef_two_ref[2:3, :] * normed + coef_two_ref[3:4, :] + field_ref[...]
    mask = jnp.where(pre > 0.0, valid, 0.0)
    acc_ref[0] += fold(jnp.maximum(pre, 0.0) * valid, clips)
    acc_ref[1] += fold(mask, clips)
    acc_ref[2] += fold(mask * normed, clips)
    size_ref[...] += fold(valid_ref[...], clips)

    @pl.when(step == pl.num_programs(0) - 1)
    def _():
        size = wide(size_ref[...], CHANNELS // 128)
        pooled_low = (acc_ref[0] / size).astype(BF)
        head = head_ref[...]
        logits = dot_nn(pooled_low, head) + bias_ref[...]
        shifted = logits - jnp.max(logits, axis=1, keepdims=True)
        log_prob = shifted - jnp.log(jnp.sum(jnp.exp(shifted), axis=1, keepdims=True))
        target = target_ref[...]
        per_clip = -jnp.sum(target * log_prob, axis=1, keepdims=True)
        keep = wide(keep_ref[...], CHANNELS // 128)
        loss = jnp.sum(keep * per_clip, axis=0, keepdims=True)
        kept = wide(coef_ref[1:2, HIDDEN:], CHANNELS // 128)
        d_logits = keep * (jnp.exp(log_prob) - target) / kept
        d_low = d_logits.astype(BF)
        grad = dot_tn(pooled_low.astype(F32), d_low.astype(F32)).astype(BF)
        half = grad.shape[0] // 2
        keep_grad_ref[...] = grad[:half]
        send_grad_ref[...] = grad[half:]
        d_pooled = dot_nt(d_low, head) / size
        dpool_ref[...] = d_pooled
        sums_one = jnp.sum(acc_ref[1] * d_pooled, axis=0, keepdims=True)
        sums_two = jnp.sum(acc_ref[2] * d_pooled, axis=0, keepdims=True)
        stats_ref[:, :CHANNELS] = to_owner_order(sums_one, order_ref[...])
        stats_ref[:, CHANNELS : 2 * CHANNELS] = to_owner_order(sums_two, order_ref[...])
        lane = lax.broadcasted_iota(jnp.int32, (1, CHANNELS), 1)
        stats_ref[:, 2 * CHANNELS :] = jnp.where(
            lane < CLASSES, jnp.sum(d_logits, axis=0, keepdims=True), loss
        )


def first_back_kernel(
    count, frames, clips, recv_ref, two_ref, field_ref, valid_ref, coef_ref, coef_two_ref, dpool_ref,
    order_ref, conv_ref, valid_out_ref, *refs
):
    pieces, refs = refs[:count], refs[count:]
    dtwo_ref, mask_ref, dpre_ref, stats_ref, w_ref, dtwo_all, back_ref, acc_ref = refs
    step = pl.program_id(0)
    per = conv_ref.shape[0]

    @pl.when(step == 0)
    def _():
        at = 0
        for piece in pieces:
            rows = piece.shape[0]
            for t in range(3):
                w_ref[t * CHANNELS + at : t * CHANNELS + at + rows, :] = piece[
                    :, CHANNELS + t * HIDDEN : CHANNELS + (t + 1) * HIDDEN
                ]
            at += rows
        total = jnp.sum(recv_ref[...], axis=0)
        each = wide(coef_ref[0:1, HIDDEN:], CHANNELS // 128)
        back_ref[0:1, :] = to_local_order(total[:, :CHANNELS], order_ref[...]) / each
        back_ref[1:2, :] = to_local_order(total[:, CHANNELS : 2 * CHANNELS], order_ref[...]) / each
        acc_ref[...] = jnp.zeros_like(acc_ref)

    @pl.when(step < frames)
    def _():
        valid = wide(valid_ref[...], CHANNELS // 128)
        gain = coef_two_ref[2:3, :]
        inverse = coef_two_ref[1:2, :]
        normed = (two_ref[...] - coef_two_ref[0:1, :]) * inverse
        pre = gain * normed + coef_two_ref[3:4, :] + field_ref[...]
        mask = jnp.where(pre > 0.0, valid, 0.0)
        spread = jnp.broadcast_to(dpool_ref[...][None], (per // clips, clips, CHANNELS))
        d_pre = mask * spread.reshape(per, CHANNELS)
        low = (
            valid * (gain * inverse) * (d_pre - back_ref[0:1, :] - normed * back_ref[1:2, :])
        ).astype(BF)
        mask_ref[...] = mask.astype(BF)
        dtwo_ref[...] = low
        dtwo_all[pl.ds(pl.multiple_of(step * per, per), per), :] = low

    def frame(last, taps):
        pieces_at = [
            dtwo_all[pl.ds(pl.multiple_of(last - k * per, per), per), :] for k in range(len(taps))
        ]
        d_first = dot_nn(
            jnp.concatenate(pieces_at, axis=1),
            w_ref[taps[0] * CHANNELS : (taps[-1] + 1) * CHANNELS, :],
        )
        normed = (conv_ref[...] - coef_ref[0:1, :HIDDEN]) * coef_ref[1:2, :HIDDEN]
        pre = coef_ref[2:3, :HIDDEN] * normed + coef_ref[3:4, :HIDDEN]
        d_pre = jnp.where(pre > 0.0, d_first, 0.0) * wide(valid_out_ref[...], HIDDEN // 128)
        dpre_ref[...] = d_pre
        acc_ref[:, :HIDDEN] += fold(d_pre, 8)
        acc_ref[:, HIDDEN:] += fold(d_pre * normed, 8)

    @pl.when(step == 1)
    def _():
        frame(per, (0, 1))

    @pl.when(jnp.logical_and(step > 1, step < frames))
    def _():
        frame(step * per, (0, 1, 2))

    @pl.when(step == frames)
    def _():
        frame((frames - 1) * per, (1, 2))
        stats_ref[...] = jnp.sum(acc_ref[...], axis=0, keepdims=True)


def conv_back_kernel(recv_ref, conv_ref, dpre_ref, valid_ref, coef_ref, out_ref, back_ref):
    @pl.when(pl.program_id(0) == 0)
    def _():
        total = jnp.sum(recv_ref[...], axis=0)
        each = wide(coef_ref[0:1, HIDDEN:], HIDDEN // 128)
        back_ref[0:1, :] = total[:, :HIDDEN] / each
        back_ref[1:2, :] = total[:, HIDDEN:] / each

    inverse = coef_ref[1:2, :HIDDEN]
    normed = (conv_ref[...] - coef_ref[0:1, :HIDDEN]) * inverse
    value = dpre_ref[...] - back_ref[0:1, :] - normed * back_ref[1:2, :]
    scale = coef_ref[2:3, :HIDDEN] * inverse
    out_ref[...] = (wide(valid_ref[...], HIDDEN // 128) * scale * value).astype(BF)


def temporal_grad_kernel(per, dtwo_ref, first_ref, keep_ref, send_ref):
    rows = dtwo_ref.shape[0]
    half = CHANNELS // 2

    def tap(low_out, low_in, size):
        grad = dot_tn(dtwo_ref[low_out : low_out + size], first_ref[low_in : low_in + size]).astype(BF)
        keep_ref[...] = grad[:half]
        send_ref[...] = grad[half:]

    step = pl.program_id(0)
    pl.when(step == 0)(lambda: tap(per, 0, rows - per))
    pl.when(step == 1)(lambda: tap(0, 0, rows))
    pl.when(step == 2)(lambda: tap(0, per, rows - per))


def spatial_grad_kernel(tap_row, per, group, cols_ref, d_ref, keep_ref, send_ref):
    rows = d_ref.shape[0]
    half = CHANNELS // 2
    if tap_row == 1:
        grad = dot_tn(cols_ref[...], d_ref[...])
    else:
        left, right = (0, group) if tap_row == 0 else (group, 0)
        size = per - group
        cols = jnp.concatenate(
            [cols_ref[f + left : f + left + size] for f in range(0, rows, per)], axis=0
        )
        back = jnp.concatenate(
            [d_ref[f + right : f + right + size] for f in range(0, rows, per)], axis=0
        )
        grad = dot_tn(cols, back)
    grad = grad.astype(BF)
    keep_ref[...] = grad[:half]
    send_ref[...] = grad[half:]


def field_back_kernel(count, tap_col, per, group, clips, d_ref, *refs):
    piece_refs, refs = refs[: 3 * count], refs[3 * count :]
    if tap_col == 1:
        out_ref, w_ref, pad_ref = refs
    elif tap_col == 0:
        acc_in_ref, out_ref, w_ref, pad_ref = refs
    else:
        (acc_in_ref, mask_ref, dpool_ref, valid_ref, x_ref, order_ref,
         out_ref, w_ref, pad_ref, grad_ref) = refs
    step = pl.program_id(0)

    @pl.when(step == 0)
    def _():
        for a in range(3):
            at = 0
            for piece in piece_refs[a * count : (a + 1) * count]:
                rows = piece.shape[0]
                w_ref[at : at + rows, a * HIDDEN : (a + 1) * HIDDEN] = piece[...]
                at += rows
        pad_ref[:group] = jnp.zeros((group, HIDDEN), BF)
        pad_ref[group + per :] = jnp.zeros((group, HIDDEN), BF)

    pad_ref[group : group + per] = d_ref[...]
    left = jnp.concatenate(
        [pad_ref[(2 - a) * group : (2 - a) * group + per] for a in range(3)], axis=1
    )
    value = dot_nt(left, w_ref[...])
    if tap_col == 1:
        out_ref[...] = value
        return
    value = value.reshape(per // group, group, CHANNELS)
    edge = jnp.zeros((per // group, clips, CHANNELS), F32)
    if tap_col == 0:
        value = jnp.concatenate([value[:, clips:], edge], axis=1)
    else:
        value = jnp.concatenate([edge, value[:, : group - clips]], axis=1)
    value = acc_in_ref[...] + value.reshape(per, CHANNELS)
    if tap_col == 0:
        out_ref[...] = value
        return
    spread = jnp.broadcast_to(dpool_ref[...][None], (per // clips, clips, CHANNELS))
    value = value + mask_ref[...].astype(F32) * spread.reshape(per, CHANNELS)
    d_entry = (value * wide(valid_ref[...], CHANNELS // 128)).astype(BF)
    grad = dot_tn(d_entry, x_ref[...])

    @pl.when(step == 0)
    def _():
        grad_ref[...] = grad

    @pl.when(step > 0)
    def _():
        grad_ref[...] += grad

    @pl.when(step == pl.num_programs(0) - 1)
    def _():
        out_ref[...] = dot_tn(order_ref[...].astype(BF), grad_ref[...].astype(BF)).astype(BF)


def split_four(devices):
    def pairs(move):
        result = []
        for source in range(devices):
            z, x, core, y = source >> 3, (source >> 2) & 1, (source >> 1) & 1, source & 1
            z, x, core, y = move(z, x, core, y)
            result.append((source, ((z * 2 + x) * 2 + core) * 2 + y))
        return result

    along_z = [pairs(lambda z, x, c, y, k=k: ((z + k) % 4, x, c, y)) for k in range(4)]
    back_z = [pairs(lambda z, x, c, y, k=k: ((z - k) % 4, x, c, y)) for k in range(4)]
    early = pairs(lambda z, x, c, y: (z, 1 - x, c, y) if c == 0 else (z, x, c, 1 - y))
    late = pairs(lambda z, x, c, y: (z, x, c, 1 - y) if c == 0 else (z, 1 - x, c, y))
    core = pairs(lambda z, x, c, y: (z, x, 1 - c, y))
    return along_z, back_z, early, late, core


class Slice:
    def __init__(self, devices):
        self.devices = devices
        self.along_z, self.back_z, self.early, self.late, self.core = split_four(devices)

    def send(self, value, pairs):
        return lax.ppermute(value, AXES, pairs)

    def order(self, rows):
        channel = jnp.arange(CHANNELS)
        block, inside = channel // rows, channel % rows
        other, j, i, k = block >> 4, (block >> 3) & 1, (block >> 2) & 1, block & 3
        at, y = lax.axis_index("dp"), lax.axis_index("outer")
        core = (at & 1) ^ other
        x = ((at >> 1) & 1) ^ jnp.where(core == 0, i, j)
        y = y ^ jnp.where(core == 0, j, i)
        z = ((at >> 2) - k) & 3
        return (((z * 2 + x) * 2 + core) * 2 + y) * rows + inside

    def gather_z(self, shard):
        return jnp.concatenate(
            [shard] + [self.send(shard, self.along_z[k]) for k in (1, 2, 3)], axis=0
        )

    def gather(self, shard):
        column = self.gather_z(shard)
        half = jnp.concatenate([column, self.send(column, self.early)], axis=0)
        rest = self.send(half, self.late)
        return [half, rest, self.send(half, self.core), self.send(rest, self.core)]

    def add_halves(self, keep, came):
        total = keep.astype(F32) + came.astype(F32)
        half = total.shape[0] // 2
        return total[:half].astype(BF), total[half:].astype(BF)

    def scatter(self, keep, send, extra=None):
        came = self.send(send, self.core)
        if extra is not None:
            keep = jnp.concatenate([extra[0], keep], axis=1)
            came = jnp.concatenate([self.send(extra[1], self.core), came], axis=1)
        keep, send = self.add_halves(keep, came)
        keep, send = self.add_halves(keep, self.send(send, self.late))
        total = keep.astype(F32) + self.send(send, self.early).astype(F32)
        rows = total.shape[0] // 4
        result = total[:rows]
        for k in (1, 2, 3):
            part = total[k * rows : (k + 1) * rows].astype(BF)
            result = result + self.send(part, self.back_z[k]).astype(F32)
        return result


class Plain:
    def __init__(self, devices):
        self.devices = devices

    def order(self, rows):
        return jnp.arange(CHANNELS)

    def gather(self, shard):
        return [lax.all_gather(shard, AXES, axis=0, tiled=True)]

    def scatter(self, keep, send, extra=None):
        value = jnp.concatenate([keep, send], axis=0)
        if extra is not None:
            value = jnp.concatenate([jnp.concatenate(extra, axis=0), value], axis=1)
        return lax.psum_scatter(value.astype(F32), AXES, scatter_dimension=0, tiled=True)


def share_rows(row, devices):
    spread = jnp.broadcast_to(row[None], (devices,) + row.shape)
    return lax.all_to_all(spread, AXES, 0, 0)


def adamw(master, grad, first, second, rate, decay, correction):
    first_new = 0.5 * first + 0.5 * grad
    second_new = 0.5 * second + 0.5 * grad * grad
    master_new = master - rate * (
        first_new / correction / (jnp.sqrt(second_new / correction) + ADAM_EPS) + decay * master
    )
    return (master_new, first_new, second_new)


def on_device(
    links,
    clip_frames,
    valid_mask,
    labels,
    clip_keep,
    step_count,
    w_entry,
    w_spatial,
    w_temporal,
    w_head,
    small_params,
    entry_first,
    entry_second,
    spatial_first,
    spatial_second,
    temporal_first,
    temporal_second,
    head_first,
    head_second,
    small_first,
    small_second,
):
    clips, frames, height, breadth, _ = clip_frames.shape
    shard = w_spatial.shape[1]
    group = breadth * clips
    per = height * group
    rows = frames * per
    shape = jax.ShapeDtypeStruct

    def flat(taps):
        return taps.astype(BF).transpose(1, 0, 2).reshape(shard, -1)

    entry_t = w_entry.T
    temporal_t = w_temporal.transpose(0, 2, 1)
    head_pad = jnp.pad(w_head.astype(BF), ((0, 0), (0, CHANNELS - CLASSES)))
    pieces_mid = links.gather(jnp.concatenate([flat(w_spatial[3:6]), entry_t.astype(BF)], axis=1))
    pieces_top = links.gather(flat(w_spatial[0:3]))
    pieces_low = links.gather(flat(w_spatial[6:9]))
    pieces_time = links.gather(jnp.concatenate([head_pad, flat(temporal_t)], axis=1))
    count = len(pieces_mid)

    index = links.order(shard)
    order = (index[:, None] == jnp.arange(CHANNELS)[None, :]).astype(F32)
    gain_one = small_params[None, :HIDDEN]
    shift_one = small_params[None, HIDDEN : 2 * HIDDEN]
    gain_two = small_params[None, 2 * HIDDEN : 2 * HIDDEN + CHANNELS]
    shift_two = small_params[None, 2 * HIDDEN + CHANNELS : 2 * HIDDEN + 2 * CHANNELS]
    bias = jnp.pad(
        small_params[None, 2 * HIDDEN + 2 * CHANNELS :],
        ((0, 0), (0, CHANNELS - CLASSES)),
        constant_values=-1e30,
    )
    x = clip_frames.transpose(1, 2, 3, 0, 4).reshape(rows, CHAN_IN)
    valid = jnp.broadcast_to(
        valid_mask.astype(F32).transpose(1, 2, 3, 0).reshape(rows, 1), (rows, 128)
    )
    keep = jnp.broadcast_to(clip_keep.astype(F32)[:, None], (clips, 128))
    lane = jnp.arange(CHANNELS)[None, :]
    target = jnp.where(
        lane < CLASSES,
        (1.0 - SMOOTHING) * (labels[:, None] == lane).astype(F32) + SMOOTHING / CLASSES,
        0.0,
    )

    def at(width, where=lambda i: i):
        return pl.BlockSpec((per, width), lambda i: (where(i), 0))

    def piece_specs(pieces):
        return [whole(p.shape) for p in pieces]

    def now(i):
        return jnp.minimum(i, frames - 1)

    def before(i):
        return jnp.maximum(i - 1, 0)

    conv_flops = 2 * rows * 3 * CHANNELS * HIDDEN

    field, cols, conv = call(
        functools.partial(entry_kernel, count, breadth, clips),
        "entry_and_middle_taps",
        (frames,),
        [at(CHAN_IN), at(128)] + piece_specs(pieces_mid),
        [at(CHANNELS), at(3 * CHANNELS), at(HIDDEN)],
        [shape((rows, CHANNELS), F32), shape((rows, 3 * CHANNELS), BF), shape((rows, HIDDEN), F32)],
        [pltpu.VMEM((3 * CHANNELS, HIDDEN), BF), pltpu.VMEM((CHANNELS, CHAN_IN), BF)],
        flops=conv_flops,
    )(x, valid, *pieces_mid)
    conv = call(
        functools.partial(spatial_kernel, count, 0, group),
        "upper_taps",
        (frames,),
        [at(3 * CHANNELS), at(HIDDEN)] + piece_specs(pieces_top),
        at(HIDDEN),
        shape((rows, HIDDEN), F32),
        [pltpu.VMEM((3 * CHANNELS, HIDDEN), BF)],
        aliases={1: 0},
        flops=conv_flops,
    )(cols, conv, *pieces_top)
    conv, stats = call(
        functools.partial(spatial_kernel, count, 2, group),
        "lower_taps",
        (frames,),
        [at(3 * CHANNELS), at(HIDDEN)] + piece_specs(pieces_low) + [at(128), whole((clips, 128))],
        [at(HIDDEN), whole((1, 2 * HIDDEN + 256))],
        [shape((rows, HIDDEN), F32), shape((1, 2 * HIDDEN + 256), F32)],
        [pltpu.VMEM((3 * CHANNELS, HIDDEN), BF), pltpu.VMEM((8, 2 * HIDDEN + 256), F32)],
        aliases={1: 0},
        flops=conv_flops,
    )(cols, conv, *pieces_low, valid, keep)
    all_stats = share_rows(stats, links.devices)

    first, two, stats_two, coef, head = call(
        functools.partial(temporal_kernel, count, frames),
        "norm_and_temporal",
        (frames + 1,),
        [whole(all_stats.shape), at(HIDDEN, now), at(128, now), at(128, before)]
        + [whole((1, HIDDEN))] * 2
        + [whole((CHANNELS, CHANNELS))]
        + piece_specs(pieces_time),
        [
            at(HIDDEN, now),
            at(CHANNELS, before),
            whole((1, 2 * CHANNELS)),
            whole((8, HIDDEN + 128)),
            whole((CHANNELS, CHANNELS)),
        ],
        [
            shape((rows, HIDDEN), BF),
            shape((rows, CHANNELS), F32),
            shape((1, 2 * CHANNELS), F32),
            shape((8, HIDDEN + 128), F32),
            shape((CHANNELS, CHANNELS), BF),
        ],
        [
            pltpu.VMEM((CHANNELS, 3 * HIDDEN), BF),
            pltpu.VMEM((rows, HIDDEN), BF),
            pltpu.VMEM((8, 2 * CHANNELS), F32),
        ],
        flops=conv_flops,
    )(all_stats, conv, valid, valid, gain_one, shift_one, order, *pieces_time)
    all_two = share_rows(stats_two, links.devices)

    half = CHANNELS // 2
    dpool, stats_three, coef_two, head_keep, head_send = call(
        functools.partial(head_kernel, clips),
        "norm_head_and_back",
        (frames,),
        [whole(all_two.shape), at(CHANNELS), at(CHANNELS), at(128), whole((8, HIDDEN + 128))]
        + [whole((1, CHANNELS))] * 2
        + [whole((CHANNELS, CHANNELS))] * 2
        + [whole((1, CHANNELS)), whole((clips, CHANNELS)), whole((clips, 128))],
        [
            whole((clips, CHANNELS)),
            whole((1, 3 * CHANNELS)),
            whole((8, CHANNELS)),
            whole((half, CHANNELS)),
            whole((half, CHANNELS)),
        ],
        [
            shape((clips, CHANNELS), F32),
            shape((1, 3 * CHANNELS), F32),
            shape((8, CHANNELS), F32),
            shape((half, CHANNELS), BF),
            shape((half, CHANNELS), BF),
        ],
        [pltpu.VMEM((3, clips, CHANNELS), F32), pltpu.VMEM((clips, 128), F32)],
    )(all_two, two, field, valid, coef, gain_two, shift_two, order, head, bias, target, keep)
    all_three = share_rows(stats_three, links.devices)

    dtwo, mask, dpre, stats_four = call(
        functools.partial(first_back_kernel, count, frames, clips),
        "temporal_back",
        (frames + 1,),
        [
            whole(all_three.shape),
            at(CHANNELS, now),
            at(CHANNELS, now),
            at(128, now),
            whole((8, HIDDEN + 128)),
            whole((8, CHANNELS)),
            whole((clips, CHANNELS)),
            whole((CHANNELS, CHANNELS)),
            at(HIDDEN, before),
            at(128, before),
        ]
        + piece_specs(pieces_time),
        [at(CHANNELS, now), at(CHANNELS, now), at(HIDDEN, before), whole((1, 2 * HIDDEN))],
        [
            shape((rows, CHANNELS), BF),
            shape((rows, CHANNELS), BF),
            shape((rows, HIDDEN), F32),
            shape((1, 2 * HIDDEN), F32),
        ],
        [
            pltpu.VMEM((3 * CHANNELS, HIDDEN), BF),
            pltpu.VMEM((rows, CHANNELS), BF),
            pltpu.VMEM((8, CHANNELS), F32),
            pltpu.VMEM((8, 2 * HIDDEN), F32),
        ],
        flops=conv_flops,
    )(all_three, two, field, valid, coef, coef_two, dpool, order, conv, valid, *pieces_time)
    all_four = share_rows(stats_four, links.devices)

    pair = [shape((half, 3 * HIDDEN), BF)] * 2
    pair_specs = [pl.BlockSpec((half, HIDDEN), lambda i: (0, i))] * 2
    time_keep, time_send = call(
        functools.partial(temporal_grad_kernel, per),
        "temporal_gradient",
        (3,),
        [whole((rows, CHANNELS)), whole((rows, HIDDEN))],
        pair_specs,
        pair,
        flops=conv_flops,
    )(dtwo, first)
    time_share = links.scatter(time_keep, time_send, (head_keep, head_send))

    dconv = call(
        conv_back_kernel,
        "spatial_norm_back",
        (frames,),
        [whole(all_four.shape), at(HIDDEN), at(HIDDEN), at(128), whole((8, HIDDEN + 128))],
        at(HIDDEN),
        shape((rows, HIDDEN), BF),
        [pltpu.VMEM((8, HIDDEN), F32)],
    )(all_four, conv, dpre, valid, coef)

    def spatial_grad(tap_row):
        return call(
            functools.partial(spatial_grad_kernel, tap_row, per, group),
            "spatial_gradient",
            (3,),
            [pl.BlockSpec((rows, CHANNELS), lambda i: (0, i)), whole((rows, HIDDEN))],
            pair_specs,
            pair,
            flops=conv_flops,
        )(cols, dconv)

    shares = {}
    for tap_row in (1, 0, 2):
        shares[tap_row] = links.scatter(*spatial_grad(tap_row))

    def field_back(tap_col, extra, extra_specs, out_spec, out_shape, scratch=()):
        pieces = pieces_top + pieces_mid + pieces_low
        return call(
            functools.partial(field_back_kernel, count, tap_col, per, group, clips),
            "field_back",
            (frames,),
            [at(HIDDEN)]
            + [pl.BlockSpec((p.shape[0], HIDDEN), lambda i: (0, tap_col)) for p in pieces]
            + extra_specs,
            out_spec,
            out_shape,
            [
                pltpu.VMEM((CHANNELS, 3 * HIDDEN), BF),
                pltpu.VMEM((per + 2 * group, HIDDEN), BF),
                *scratch,
            ],
            flops=conv_flops,
        )(dconv, *pieces, *extra)

    partial = shape((rows, CHANNELS), F32)
    back = field_back(1, [], [], at(CHANNELS), partial)
    back = field_back(0, [back], [at(CHANNELS)], at(CHANNELS), partial)
    grad_entry = field_back(
        2,
        [back, mask, dpool, valid, x, order],
        [
            at(CHANNELS),
            at(CHANNELS),
            whole((clips, CHANNELS)),
            at(128),
            at(CHAN_IN),
            whole((CHANNELS, CHANNELS)),
        ],
        whole((CHANNELS, CHAN_IN)),
        shape((CHANNELS, CHAN_IN), BF),
        [pltpu.VMEM((CHANNELS, CHAN_IN), F32)],
    )
    entry_parts = lax.all_to_all(grad_entry.reshape(links.devices, shard, CHAN_IN), AXES, 0, 0)
    entry_share = jnp.sum(entry_parts.astype(F32), axis=0)

    def taps(share):
        return share.reshape(shard, 3, HIDDEN).transpose(1, 0, 2)

    correction = 1.0 - jnp.power(0.5, step_count[0].astype(F32))
    total_three = jnp.sum(all_three, axis=(0, 1))
    total_four = jnp.sum(all_four, axis=(0, 1))
    small_grad = jnp.concatenate(
        [
            total_four[HIDDEN:],
            total_four[:HIDDEN],
            total_three[CHANNELS : 2 * CHANNELS],
            total_three[:CHANNELS],
            total_three[2 * CHANNELS : 2 * CHANNELS + CLASSES],
        ]
    )
    loss = total_three[2 * CHANNELS + CLASSES] / coef[1, HIDDEN]
    spatial_grad_share = jnp.concatenate([taps(shares[a]) for a in range(3)], axis=0)
    temporal_share = taps(time_share[:, CHANNELS:]).transpose(0, 2, 1)
    entry_out = adamw(
        w_entry, entry_share.T, entry_first, entry_second, 0.06, DECAY_RATE, correction
    )
    spatial_out = adamw(
        w_spatial, spatial_grad_share, spatial_first, spatial_second, 0.02, DECAY_RATE, correction
    )
    temporal_out = adamw(
        w_temporal, temporal_share, temporal_first, temporal_second, 0.02, DECAY_RATE, correction
    )
    head_out = adamw(
        w_head, time_share[:, :CLASSES], head_first, head_second, 0.05, DECAY_RATE, correction
    )
    small_out = adamw(small_params, small_grad, small_first, small_second, 0.5, 0.0, correction)
    return (
        loss,
        *entry_out,
        *spatial_out,
        *temporal_out,
        *head_out,
        *small_out,
        entry_out[0].astype(BF),
        spatial_out[0].astype(BF),
        temporal_out[0].astype(BF),
        head_out[0].astype(BF),
    )


def solution(mesh):
    devices = mesh.shape["dp"] * mesh.shape["outer"]
    small_slice = mesh.shape["dp"] == 16 and mesh.shape["outer"] == 2
    links = Slice(devices) if small_slice else Plain(devices)
    both = ("dp", "outer")
    entry, spatial, temporal, head = (
        P(None, both),
        P(None, both, None),
        P(None, None, both),
        P(both, None),
    )
    placed = (
        P(both, None, None, None, None),
        P(both, None, None, None),
        P(both),
        P(both),
        P(),
        entry,
        spatial,
        temporal,
        head,
        P(),
        entry,
        entry,
        spatial,
        spatial,
        temporal,
        temporal,
        head,
        head,
        P(),
        P(),
    )
    return jax.shard_map(
        functools.partial(on_device, links),
        mesh=mesh,
        in_specs=placed,
        out_specs=(
            P(),
            *([entry] * 3),
            *([spatial] * 3),
            *([temporal] * 3),
            *([head] * 3),
            P(),
            P(),
            P(),
            entry,
            spatial,
            temporal,
            head,
        ),
        check_vma=False,
    )
```

time: 1140 us -> 479 us (0.42)
  waiting for transfers between devices: 502 us -> 161 us
  blocking collectives: 303 us -> 0 us
  Pallas kernels: 0 us -> 162 us
  matrix products: 143 us -> 0 us
  other arithmetic: 92 us -> 18 us
  starting transfers between devices: 0.25 us -> 72.3 us
  local copies, waits for them, and re-layouts: 71.4 us -> 50.6 us
  between operations: 18.3 us -> 5.3 us
    reduce_scatter x4 -> x0, waiting for transfers between devices: 502 us -> none  [the longest x1 223 us: on_device(): lax.psum_scatter(grad_spatial, ('dp', 'outer'), scatter_dimension=1, tile...]
    psum x4 -> x0, blocking collectives: 162 us -> none  [the longest x2 81.5 us: on_device(): lax.psum((jnp.sum(d_normed_two, axis=0), jnp.sum(d_normed_two * normed_tw...]
    pallas_call x0 -> x14, Pallas kernels: none -> 162 us  [the longest x3 37.1 us: field_back(): call(functools.partial(field_back_kernel, count, tap_col, per, group, cli...]
    dot_general x11 -> x0, matrix products: 143 us -> none  [the longest x4 47.8 us: contract_first(): lax.dot_general(operand, factor, (((0,), (0,)), ((), ())), preferred_elem...]
    all_gather x2 -> x0, blocking collectives: 141 us -> none  [the longest x1 71.8 us: on_device(): lax.all_gather(w_entry.astype(jnp.bfloat16), ('dp', 'outer'), axis=1, til...]
    ppermute x0 -> x53, waiting for transfers between devices: none -> 128 us  [send(): return lax.ppermute(value, AXES, pairs)]
    ppermute x0 -> x53, starting transfers between devices: none -> 50.4 us  [send(): return lax.ppermute(value, AXES, pairs)]
    dot_general x2 -> x0, local copies, waits for them, and re-layouts: 42.1 us -> none  [contract_first(): lax.dot_general(operand, factor, (((0,), (0,)), ((), ())), preferred_elem...]
  transfers between devices with their start and end apart: 6 -> 58, of which waited for: 4 -> 24; matrix products, arithmetic and copies ran while one was open for 13% -> 6% of each run, Pallas kernels for 0% -> 29%
where the time goes in v1:
time: 479 us; the launch traced here: 469 us
  Pallas kernels  162 us (34%)
  waiting for transfers between devices  161 us (34%)
  starting transfers between devices  72.3 us (15%)
  local copies, waits for them, and re-layouts  50.6 us (11%)
  other arithmetic  18 us (4%)
  between operations  5.3 us (1%)
    ppermute x53, waiting for transfers between devices, send(): return lax.ppermute(value, AXES, pairs)  128 us
    ppermute x53, starting transfers between devices, send(): return lax.ppermute(value, AXES, pairs)  50.4 us
    unnamed x135, local copies, waits for them, and re-layouts  40.5 us
    pallas_call x3, Pallas kernels, field_back(): call(functools.partial(field_back_kernel, count, tap_col, per, group, cli...  37.1 us
    all_to_all x4, waiting for transfers between devices, share_rows(): return lax.all_to_all(spread, AXES, 0, 0)  28.2 us
    pallas_call x3, Pallas kernels, spatial_grad(): call(functools.partial(spatial_grad_kernel, tap_row, per, group), 'spatia...  27.1 us
    pallas_call x1, Pallas kernels, on_device(): call(functools.partial(first_back_kernel, count, frames, clips), 'tempora...  18 us
    all_to_all x4, starting transfers between devices, share_rows(): return lax.all_to_all(spread, AXES, 0, 0)  15.7 us
  transfers between devices with their start and end apart: 58, of which 24 were waited for; matrix products, arithmetic and copies ran while one was open for 6% of the time, Pallas kernels for 29%

profile of v1, /device:TPU:0, one launch (start us, length us, event | category | flops | bytes accessed | tf_op | source)
XLA Modules:
  0.0 469.4 jit_solution(10793120511960379723)
XLA Ops:
  11.5 7.9 %collective-permute-done.7 = bf16[16,3456]{1,0:T(8,128)(2,1)S(1)} collective-permute-done((bf16[16,3456]{1,0:T(8,128)(2,1)S(1)}, bf16[16,3456]{1,0:T(8,128)(2,1)S(1)}, u32[]{:S(2)}, u32[]{:S(2)}) %collective-permute-start.7) | collective-permute-done | bytes 110624 | tf_op jit(solution)/shard_map/ppermute | solution.py:478
  51.6 12.9 %collective-permute-done.3 = bf16[64,3712]{1,0:T(8,128)(2,1)S(1)} collective-permute-done((bf16[64,3712]{1,0:T(8,128)(2,1)S(1)}, bf16[64,3712]{1,0:T(8,128)(2,1)S(1)}, u32[]{:S(2)}, u32[]{:S(2)}) %collective-permute-start.3) | collective-permute-done | bytes 475168 | tf_op jit(solution)/shard_map/ppermute | solution.py:478
  69.0 9.4 %collective-permute-done.4.refs_1_.refs_5_ = bf16[128,3712]{1,0:T(8,128)(2,1)} collective-permute-done((bf16[128,3712]{1,0:T(8,128)(2,1)S(1)}, bf16[128,3712]{1,0:T(8,128)(2,1)}, u32[]{:S(2)}, u32[]{:S(2)}) %collective-permute-start.4) | collective-permute-done | bytes 950304 | tf_op jit(solution)/shard_map/ppermute | solution.py:478
  87.9 9.3 %collective-permute-done.18.refs_1_.refs_9_ = bf16[128,3456]{1,0:T(8,128)(2,1)S(1)} collective-permute-done((bf16[128,3456]{1,0:T(8,128)(2,1)S(1)}, bf16[128,3456]{1,0:T(8,128)(2,1)S(1)}, u32[]{:S(2)}, u32[]{:S(2)}) %collective-permute-start.18) | collective-permute-done | bytes 884768 | tf_op jit(solution)/shard_map/ppermute | solution.py:478
  103.1 14.0 %entry_and_middle_taps.1 = (f32[2048,512]{1,0:T(8,128)S(1)}, bf16[2048,1536]{1,0:T(8,128)(2,1)}, f32[2048,1152]{1,0:T(8,128)}) custom-call(bf16[2048,256]{1,0:T(8,128)(2,1)S(1)} %bitcast.71, f32[2048,128]{1,0:T(8,128)S(1)} %broadcast_in_dim.75.valid_ref.refs_4_.valid_out_ref.refs_15_, bf16[128,3712]{1,0:T(8,128)(2,1)S(1)} %copy-done.24, ...), custom_call_target="tpu_custom_call" | custom-call | flops 7247757312 | bytes 20971520 | tf_op jit(solution)/shard_map/entry_and_middle_taps/pallas_call | solution.py:633
  122.4 12.3 %upper_taps.1.conv_ref = f32[2048,1152]{1,0:T(8,128)} custom-call(bf16[2048,1536]{1,0:T(8,128)(2,1)S(1)} %copy-done, f32[2048,1152]{1,0:T(8,128)} %get-tuple-element.48.conv_ref, bf16[128,3456]{1,0:T(8,128)(2,1)S(1)} %constant_dynamic-update-slice_fusion.5.refs_0_, ...), custom_call_target="tpu_custom_call", output_to_operand_aliasing={{}: (1, {})} | custom-call | flops 7247757312 | bytes 20971520 | tf_op jit(solution)/shard_map/upper_taps/pallas_call | solution.py:643
  134.8 13.7 %lower_taps.1 = (f32[2048,1152]{1,0:T(8,128)}, f32[1,2560]{1,0:T(1,128)S(1)}) custom-call(bf16[2048,1536]{1,0:T(8,128)(2,1)S(1)} %copy-done, f32[2048,1152]{1,0:T(8,128)} %upper_taps.1.conv_ref, bf16[128,3456]{1,0:T(8,128)(2,1)S(1)} %copy-done.27, bf16[128,3456]{1,0:T(8,128)(2,1)S(1)} %copy-done.32, ...), custom_call_target="tpu_custom_call", output_to_operand_aliasing={{0}: (1, {})} | custom-call | flops 7247757312 | bytes 20971520 | tf_op jit(solution)/shard_map/lower_taps/pallas_call | solution.py:654
  157.0 11.5 %all-to-all-done.recv_ref = f32[32,1,2560]{2,1,0:T(1,128)} async-done(((f32[32,1,2560]{2,1,0:T(1,128)}), f32[32,1,2560]{2,1,0:T(1,128)}, u32[]{:S(2)}, u32[]{:S(2)}) %all-to-all-start) | async-done | bytes 327712 | tf_op jit(solution)/shard_map/all_to_all | solution.py:542
  168.4 15.3 %norm_and_temporal.1 = (bf16[2048,1152]{1,0:T(8,128)(2,1)}, f32[2048,512]{1,0:T(8,128)S(1)}, f32[1,1024]{1,0:T(1,128)S(1)}, f32[8,1280]{1,0:T(8,128)S(1)}, bf16[512,512]{1,0:T(8,128)(2,1)S(1)}) custom-call(f32[32,1,2560]{2,1,0:T(1,128)} %all-to-all-done.recv_ref, f32[2048,1152]{1,0:T(8,128)} %get-tuple-element.50.conv_ref, ...), custom_call_target="tpu_custom_call" | custom-call | flops 7247757312 | bytes 20971520 | tf_op jit(solution)/shard_map/norm_and_temporal/pallas_call | solution.py:667
  190.0 8.5 %all-to-all-done.1.recv_ref = f32[32,1,1024]{2,1,0:T(1,128)S(1)} async-done(((f32[32,1,1024]{2,1,0:T(1,128)}), f32[32,1,1024]{2,1,0:T(1,128)S(1)}, u32[]{:S(2)}, u32[]{:S(2)}) %all-to-all-start.1) | async-done | bytes 131104 | tf_op jit(solution)/shard_map/all_to_all | solution.py:542
  203.9 8.2 %norm_head_and_back.1 = (f32[8,512]{1,0:T(8,128)S(1)}, f32[1,1536]{1,0:T(1,128)S(1)}, f32[8,512]{1,0:T(8,128)S(1)}, bf16[256,512]{1,0:T(8,128)(2,1)S(1)}, bf16[256,512]{1,0:T(8,128)(2,1)}) custom-call(f32[32,1,1024]{2,1,0:T(1,128)S(1)} %all-to-all-done.1.recv_ref, f32[2048,512]{1,0:T(8,128)S(1)} %copy-done.6, f32[2048,512]{1,0:T(8,128)S(1)} %copy-done.4, ...), custom_call_target="tpu_custom_call" | custom-call | bytes 20971520 | tf_op jit(solution)/shard_map/norm_head_and_back/pallas_call | solution.py:699
  218.0 8.2 %all-to-all-done.2.recv_ref = f32[32,1,1536]{2,1,0:T(1,128)S(1)} async-done(((f32[32,1,1536]{2,1,0:T(1,128)}), f32[32,1,1536]{2,1,0:T(1,128)S(1)}, u32[]{:S(2)}, u32[]{:S(2)}) %all-to-all-start.2) | async-done | bytes 196640 | tf_op jit(solution)/shard_map/all_to_all | solution.py:542
  226.3 18.0 %temporal_back.1 = (bf16[2048,512]{1,0:T(8,128)(2,1)S(1)}, bf16[2048,512]{1,0:T(8,128)(2,1)S(1)}, f32[2048,1152]{1,0:T(8,128)}, f32[1,2304]{1,0:T(1,128)S(1)}) custom-call(f32[32,1,1536]{2,1,0:T(1,128)S(1)} %all-to-all-done.2.recv_ref, f32[2048,512]{1,0:T(8,128)} %copy-done.5, f32[2048,512]{1,0:T(8,128)} %copy-done.3, ...), custom_call_target="tpu_custom_call" | custom-call | flops 7247757312 | bytes 20971520 | tf_op jit(solution)/shard_map/temporal_back/pallas_call | solution.py:725
  254.5 8.4 %temporal_gradient.1 = (bf16[256,3456]{1,0:T(8,128)(2,1)S(1)}, bf16[256,3456]{1,0:T(8,128)(2,1)}) custom-call(bf16[2048,512]{1,0:T(8,128)(2,1)S(1)} %copy-done.40, bf16[2048,1152]{1,0:T(8,128)(2,1)S(1)} %copy-done.41), custom_call_target="tpu_custom_call" | custom-call | flops 7247757312 | bytes 20971520 | tf_op jit(solution)/shard_map/temporal_gradient/pallas_call | solution.py:761
  266.4 7.7 %spatial_norm_back.1.d_ref = bf16[2048,1152]{1,0:T(8,128)(2,1)S(1)} custom-call(f32[32,1,2304]{2,1,0:T(1,128)S(1)} %all-to-all-done.3.recv_ref, f32[2048,1152]{1,0:T(8,128)} %get-tuple-element.50.conv_ref, f32[2048,1152]{1,0:T(8,128)} %get-tuple-element.60.dpre_ref, f32[2048,128]{1,0:T(8,128)S(1)} %broadcast_in_dim.75.valid_ref.refs_4_.valid_out_ref.refs_15_, ...), custom_call_target="tpu_custom_call" | custom-call | bytes 20971520 | tf_op jit(solution)/shard_map/spatial_norm_back/pallas_call | solution.py:772
  276.9 9.1 %spatial_gradient.3 = (bf16[256,3456]{1,0:T(8,128)(2,1)S(1)}, bf16[256,3456]{1,0:T(8,128)(2,1)}) custom-call(bf16[2048,1536]{1,0:T(8,128)(2,1)S(1)} %copy-done.1, bf16[2048,1152]{1,0:T(8,128)(2,1)S(1)} %spatial_norm_back.1.d_ref), custom_call_target="tpu_custom_call" | custom-call | flops 7247757312 | bytes 20971520 | tf_op jit(solution)/shard_map/spatial_gradient/pallas_call | solution.py:783
  287.3 9.4 %spatial_gradient.4 = (bf16[256,3456]{1,0:T(8,128)(2,1)S(1)}, bf16[256,3456]{1,0:T(8,128)(2,1)S(1)}) custom-call(bf16[2048,1536]{1,0:T(8,128)(2,1)S(1)} %copy-done.1, bf16[2048,1152]{1,0:T(8,128)(2,1)S(1)} %spatial_norm_back.1.d_ref), custom_call_target="tpu_custom_call" | custom-call | flops 7247757312 | bytes 20971520 | tf_op jit(solution)/shard_map/spatial_gradient/pallas_call | solution.py:783
  298.0 8.6 %spatial_gradient.5 = (bf16[256,3456]{1,0:T(8,128)(2,1)S(1)}, bf16[256,3456]{1,0:T(8,128)(2,1)S(1)}) custom-call(bf16[2048,1536]{1,0:T(8,128)(2,1)S(1)} %copy-done.1, bf16[2048,1152]{1,0:T(8,128)(2,1)S(1)} %spatial_norm_back.1.d_ref), custom_call_target="tpu_custom_call" | custom-call | flops 7247757312 | bytes 20971520 | tf_op jit(solution)/shard_map/spatial_gradient/pallas_call | solution.py:783
  308.8 11.6 %field_back.3.refs_12_ = f32[2048,512]{1,0:T(8,128)} custom-call(bf16[2048,1152]{1,0:T(8,128)(2,1)} %copy-done.2, bf16[128,3456]{1,0:T(8,128)(2,1)S(1)} %constant_dynamic-update-slice_fusion.5.refs_0_, bf16[128,3456]{1,0:T(8,128)(2,1)S(1)} %copy-done.17, bf16[128,3456]{1,0:T(8,128)(2,1)} %collective-permute-done.12.refs_2_, ...), custom_call_target="tpu_custom_call" | custom-call | flops 7247757312 | bytes 20971520 | tf_op jit(solution)/shard_map/field_back/pallas_call | solution.py:799
  320.4 12.1 %field_back.4.refs_12_ = f32[2048,512]{1,0:T(8,128)} custom-call(bf16[2048,1152]{1,0:T(8,128)(2,1)} %copy-done.2, bf16[128,3456]{1,0:T(8,128)(2,1)S(1)} %constant_dynamic-update-slice_fusion.5.refs_0_, bf16[128,3456]{1,0:T(8,128)(2,1)S(1)} %copy-done.17, bf16[128,3456]{1,0:T(8,128)(2,1)} %collective-permute-done.12.refs_2_, ...), custom_call_target="tpu_custom_call" | custom-call | flops 7247757312 | bytes 20971520 | tf_op jit(solution)/shard_map/field_back/pallas_call | solution.py:799
  332.5 13.5 %field_back.5 = bf16[512,256]{1,0:T(8,128)(2,1)S(1)} custom-call(bf16[2048,1152]{1,0:T(8,128)(2,1)} %copy-done.2, bf16[128,3456]{1,0:T(8,128)(2,1)S(1)} %constant_dynamic-update-slice_fusion.5.refs_0_, bf16[128,3456]{1,0:T(8,128)(2,1)S(1)} %copy-done.17, bf16[128,3456]{1,0:T(8,128)(2,1)} %collective-permute-done.12.refs_2_, ...), custom_call_target="tpu_custom_call" | custom-call | flops 7247757312 | bytes 20971520 | tf_op jit(solution)/shard_map/field_back/pallas_call | solution.py:799
  385.5 14.3 %collective-permute-done.29 = bf16[128,3456]{1,0:T(8,128)(2,1)S(1)} collective-permute-done((bf16[128,3456]{1,0:T(8,128)(2,1)S(1)}, bf16[128,3456]{1,0:T(8,128)(2,1)S(1)}, u32[]{:S(2)}, u32[]{:S(2)}) %collective-permute-start.29) | collective-permute-done | bytes 884768 | tf_op jit(solution)/shard_map/ppermute | solution.py:478
  400.4 13.7 %collective-permute-done.35 = bf16[128,3456]{1,0:T(8,128)(2,1)S(1)} collective-permute-done((bf16[128,3456]{1,0:T(8,128)(2,1)S(1)}, bf16[128,3456]{1,0:T(8,128)(2,1)S(1)}, u32[]{:S(2)}, u32[]{:S(2)}) %collective-permute-start.35) | collective-permute-done | bytes 884768 | tf_op jit(solution)/shard_map/ppermute | solution.py:478
  417.1 11.2 %collective-permute-done.41 = bf16[128,3456]{1,0:T(8,128)(2,1)S(1)} collective-permute-done((bf16[128,3456]{1,0:T(8,128)(2,1)S(1)}, bf16[128,3456]{1,0:T(8,128)(2,1)S(1)}, u32[]{:S(2)}, u32[]{:S(2)}) %collective-permute-start.41) | collective-permute-done | bytes 884768 | tf_op jit(solution)/shard_map/ppermute | solution.py:478
  (327 shorter events, 195.4 us)
Async XLA Ops:
  2.6 39.9 %collective-permute-start = (bf16[16,3712]{1,0:T(8,128)(2,1)S(1)}, bf16[16,3712]{1,0:T(8,128)(2,1)S(1)}, u32[]{:S(2)}, u32[]{:S(2)}) collective-permute-start(bf16[16,3712]{1,0:T(8,128)(2,1)S(1)} %get-tuple-element.138), channel_id=1, source_target_pairs={{0,8},{1,9},{2,10},{3,11},{4,12},{5,13},{6,14},{7,15},{8,16},{9,17... | collective-permute-start | bytes 356360 | tf_op jit(solution)/shard_map/ppermute | solution.py:478
  5.7 38.8 %collective-permute-start.1 = (bf16[16,3712]{1,0:T(8,128)(2,1)S(1)}, bf16[16,3712]{1,0:T(8,128)(2,1)S(1)}, u32[]{:S(2)}, u32[]{:S(2)}) collective-permute-start(bf16[16,3712]{1,0:T(8,128)(2,1)S(1)} %get-tuple-element.138), channel_id=1, source_target_pairs={{0,16},{1,17},{2,18},{3,19},{4,20},{5,21},{6,22},{7,23},{8,24},{9,... | collective-permute-start | bytes 356360 | tf_op jit(solution)/shard_map/ppermute | solution.py:478
  8.3 37.8 %collective-permute-start.2 = (bf16[16,3712]{1,0:T(8,128)(2,1)S(1)}, bf16[16,3712]{1,0:T(8,128)(2,1)S(1)}, u32[]{:S(2)}, u32[]{:S(2)}) collective-permute-start(bf16[16,3712]{1,0:T(8,128)(2,1)S(1)} %get-tuple-element.138), channel_id=1, source_target_pairs={{0,24},{1,25},{2,26},{3,27},{4,28},{5,29},{6,30},{7,31},{8,0},{9,1... | collective-permute-start | bytes 356360 | tf_op jit(solution)/shard_map/ppermute | solution.py:478
  44.5 22.2 %collective-permute-start.10 = (bf16[64,3456]{1,0:T(8,128)(2,1)S(1)}, bf16[64,3456]{1,0:T(8,128)(2,1)S(1)}, u32[]{:S(2)}, u32[]{:S(2)}) collective-permute-start(bf16[64,3456]{1,0:T(8,128)(2,1)S(1)} %pad_maximum_fusion.3), channel_id=1, source_target_pairs={{0,4},{1,5},{2,3},{3,2},{4,0},{5,1},{6,7},{7,6},{8,12},{9,13},{10,... | collective-permute-start | bytes 1327112 | tf_op jit(solution)/shard_map/ppermute | solution.py:478
  49.4 29.8 %collective-permute-start.24 = (bf16[64,3968]{1,0:T(8,128)(2,1)S(1)}, bf16[64,3968]{1,0:T(8,128)(2,1)S(1)}, u32[]{:S(2)}, u32[]{:S(2)}) collective-permute-start(bf16[64,3968]{1,0:T(8,128)(2,1)S(1)} %pad_maximum_fusion.1), channel_id=1, source_target_pairs={{0,4},{1,5},{2,3},{3,2},{4,0},{5,1},{6,7},{7,6},{8,12},{9,13},{10,... | collective-permute-start | bytes 1523720 | tf_op jit(solution)/shard_map/ppermute | solution.py:478
  67.4 29.8 %collective-permute-start.18 = (bf16[128,3456]{1,0:T(8,128)(2,1)S(1)}, bf16[128,3456]{1,0:T(8,128)(2,1)S(1)}, u32[]{:S(2)}, u32[]{:S(2)}) collective-permute-start(bf16[128,3456]{1,0:T(8,128)(2,1)S(1)} %constant_dynamic-update-slice_fusion.10.refs_0_.refs_8_), channel_id=1, source_target_pairs={{0,1},{1,0},{2,6},{3,7},{4,5},{5,4},{6,2},{7,3},{8,9},{9,8},{10,14... | collective-permute-start | bytes 2654216 | tf_op jit(solution)/shard_map/ppermute | solution.py:478
  69.0 32.0 %collective-permute-start.5 = (bf16[128,3712]{1,0:T(8,128)(2,1)S(1)}, bf16[128,3712]{1,0:T(8,128)(2,1)}, u32[]{:S(2)}, u32[]{:S(2)}) collective-permute-start(bf16[128,3712]{1,0:T(8,128)(2,1)S(1)} %constant_dynamic-update-slice_fusion.refs_0_.refs_4_), channel_id=1, source_target_pairs={{0,2},{1,3},{2,0},{3,1},{4,6},{5,7},{6,4},{7,5},{8,10},{9,11},{10,... | collective-permute-start | bytes 2850824 | tf_op jit(solution)/shard_map/ppermute | solution.py:478
  78.4 22.9 %collective-permute-start.6 = (bf16[128,3712]{1,0:T(8,128)(2,1)}, bf16[128,3712]{1,0:T(8,128)(2,1)}, u32[]{:S(2)}, u32[]{:S(2)}) collective-permute-start(bf16[128,3712]{1,0:T(8,128)(2,1)} %collective-permute-done.4.refs_1_.refs_5_), channel_id=1, source_target_pairs={{0,2},{1,3},{2,0},{3,1},{4,6},{5,7},{6,4},{7,5},{8,10},{9,11},{10,... | collective-permute-start | bytes 2850824 | tf_op jit(solution)/shard_map/ppermute | solution.py:478
  80.0 39.3 %collective-permute-start.25 = (bf16[128,3968]{1,0:T(8,128)(2,1)}, bf16[128,3968]{1,0:T(8,128)(2,1)}, u32[]{:S(2)}, u32[]{:S(2)}) collective-permute-start(bf16[128,3968]{1,0:T(8,128)(2,1)} %constant_dynamic-update-slice_fusion.15.refs_0_), channel_id=1, source_target_pairs={{0,1},{1,0},{2,6},{3,7},{4,5},{5,4},{6,2},{7,3},{8,9},{9,8},{10,14... | collective-permute-start | bytes 3047432 | tf_op jit(solution)/shard_map/ppermute | solution.py:478
  87.8 31.3 %collective-permute-start.12 = (bf16[128,3456]{1,0:T(8,128)(2,1)S(1)}, bf16[128,3456]{1,0:T(8,128)(2,1)}, u32[]{:S(2)}, u32[]{:S(2)}) collective-permute-start(bf16[128,3456]{1,0:T(8,128)(2,1)S(1)} %constant_dynamic-update-slice_fusion.5.refs_0_), channel_id=1, source_target_pairs={{0,2},{1,3},{2,0},{3,1},{4,6},{5,7},{6,4},{7,5},{8,10},{9,11},{10,... | collective-permute-start | bytes 2654216 | tf_op jit(solution)/shard_map/ppermute | solution.py:478
  98.2 21.4 %collective-permute-start.13 = (bf16[128,3456]{1,0:T(8,128)(2,1)S(1)}, bf16[128,3456]{1,0:T(8,128)(2,1)}, u32[]{:S(2)}, u32[]{:S(2)}) collective-permute-start(bf16[128,3456]{1,0:T(8,128)(2,1)S(1)} %collective-permute-done.11.refs_1_), channel_id=1, source_target_pairs={{0,2},{1,3},{2,0},{3,1},{4,6},{5,7},{6,4},{7,5},{8,10},{9,11},{10,... | collective-permute-start | bytes 2654216 | tf_op jit(solution)/shard_map/ppermute | solution.py:478
  101.0 33.7 %collective-permute-start.19 = (bf16[128,3456]{1,0:T(8,128)(2,1)S(1)}, bf16[128,3456]{1,0:T(8,128)(2,1)S(1)}, u32[]{:S(2)}, u32[]{:S(2)}) collective-permute-start(bf16[128,3456]{1,0:T(8,128)(2,1)S(1)} %copy-done.27), channel_id=1, source_target_pairs={{0,2},{1,3},{2,0},{3,1},{4,6},{5,7},{6,4},{7,5},{8,10},{9,11},{10,... | collective-permute-start | bytes 2654216 | tf_op jit(solution)/shard_map/ppermute | solution.py:478
  101.4 33.4 %collective-permute-start.20 = (bf16[128,3456]{1,0:T(8,128)(2,1)S(1)}, bf16[128,3456]{1,0:T(8,128)(2,1)S(1)}, u32[]{:S(2)}, u32[]{:S(2)}) collective-permute-start(bf16[128,3456]{1,0:T(8,128)(2,1)S(1)} %copy-done.32), channel_id=1, source_target_pairs={{0,2},{1,3},{2,0},{3,1},{4,6},{5,7},{6,4},{7,5},{8,10},{9,11},{10,... | collective-permute-start | bytes 2654216 | tf_op jit(solution)/shard_map/ppermute | solution.py:478
  119.1 37.9 %collective-permute-start.26 = (bf16[128,3968]{1,0:T(8,128)(2,1)}, bf16[128,3968]{1,0:T(8,128)(2,1)}, u32[]{:S(2)}, u32[]{:S(2)}) collective-permute-start(bf16[128,3968]{1,0:T(8,128)(2,1)} %constant_dynamic-update-slice_fusion.15.refs_0_), channel_id=1, source_target_pairs={{0,2},{1,3},{2,0},{3,1},{4,6},{5,7},{6,4},{7,5},{8,10},{9,11},{10,... | collective-permute-start | bytes 3047432 | tf_op jit(solution)/shard_map/ppermute | solution.py:478
  119.4 37.6 %collective-permute-start.27 = (bf16[128,3968]{1,0:T(8,128)(2,1)}, bf16[128,3968]{1,0:T(8,128)(2,1)}, u32[]{:S(2)}, u32[]{:S(2)}) collective-permute-start(bf16[128,3968]{1,0:T(8,128)(2,1)} %collective-permute-done.25.refs_1_), channel_id=1, source_target_pairs={{0,2},{1,3},{2,0},{3,1},{4,6},{5,7},{6,4},{7,5},{8,10},{9,11},{10,... | collective-permute-start | bytes 3047432 | tf_op jit(solution)/shard_map/ppermute | solution.py:478
  217.8 150.0 %collective-permute-start.46 = (bf16[256,512]{1,0:T(8,128)(2,1)}, bf16[256,512]{1,0:T(8,128)(2,1)}, u32[]{:S(2)}, u32[]{:S(2)}) collective-permute-start(bf16[256,512]{1,0:T(8,128)(2,1)} %get-tuple-element.72), channel_id=1, source_target_pairs={{0,2},{1,3},{2,0},{3,1},{4,6},{5,7},{6,4},{7,5},{8,10},{9,11},{10,... | collective-permute-start | bytes 786440 | tf_op jit(solution)/shard_map/ppermute | solution.py:478
  264.1 103.7 %collective-permute-start.47 = (bf16[256,3456]{1,0:T(8,128)(2,1)}, bf16[256,3456]{1,0:T(8,128)(2,1)}, u32[]{:S(2)}, u32[]{:S(2)}) collective-permute-start(bf16[256,3456]{1,0:T(8,128)(2,1)} %get-tuple-element.73), channel_id=1, source_target_pairs={{0,2},{1,3},{2,0},{3,1},{4,6},{5,7},{6,4},{7,5},{8,10},{9,11},{10,... | collective-permute-start | bytes 5308424 | tf_op jit(solution)/shard_map/ppermute | solution.py:478
  306.6 64.6 %collective-permute-start.28 = (bf16[256,3456]{1,0:T(8,128)(2,1)}, bf16[256,3456]{1,0:T(8,128)(2,1)}, u32[]{:S(2)}, u32[]{:S(2)}) collective-permute-start(bf16[256,3456]{1,0:T(8,128)(2,1)} %get-tuple-element.63), channel_id=1, source_target_pairs={{0,2},{1,3},{2,0},{3,1},{4,6},{5,7},{6,4},{7,5},{8,10},{9,11},{10,... | collective-permute-start | bytes 5308424 | tf_op jit(solution)/shard_map/ppermute | solution.py:478
  373.8 26.0 %collective-permute-start.29 = (bf16[128,3456]{1,0:T(8,128)(2,1)S(1)}, bf16[128,3456]{1,0:T(8,128)(2,1)S(1)}, u32[]{:S(2)}, u32[]{:S(2)}) collective-permute-start(bf16[128,3456]{1,0:T(8,128)(2,1)S(1)} %slice.232), channel_id=1, source_target_pairs={{0,1},{1,0},{2,6},{3,7},{4,5},{5,4},{6,2},{7,3},{8,9},{9,8},{10,14... | collective-permute-start | bytes 2654216 | tf_op jit(solution)/shard_map/ppermute | solution.py:478
  377.3 36.8 %collective-permute-start.35 = (bf16[128,3456]{1,0:T(8,128)(2,1)S(1)}, bf16[128,3456]{1,0:T(8,128)(2,1)S(1)}, u32[]{:S(2)}, u32[]{:S(2)}) collective-permute-start(bf16[128,3456]{1,0:T(8,128)(2,1)S(1)} %slice.240), channel_id=1, source_target_pairs={{0,1},{1,0},{2,6},{3,7},{4,5},{5,4},{6,2},{7,3},{8,9},{9,8},{10,14... | collective-permute-start | bytes 2654216 | tf_op jit(solution)/shard_map/ppermute | solution.py:478
  379.2 49.1 %collective-permute-start.41 = (bf16[128,3456]{1,0:T(8,128)(2,1)S(1)}, bf16[128,3456]{1,0:T(8,128)(2,1)S(1)}, u32[]{:S(2)}, u32[]{:S(2)}) collective-permute-start(bf16[128,3456]{1,0:T(8,128)(2,1)S(1)} %slice.248), channel_id=1, source_target_pairs={{0,1},{1,0},{2,6},{3,7},{4,5},{5,4},{6,2},{7,3},{8,9},{9,8},{10,14... | collective-permute-start | bytes 2654216 | tf_op jit(solution)/shard_map/ppermute | solution.py:478
  385.2 29.4 %collective-permute-start.49 = (bf16[64,3968]{1,0:T(8,128)(2,1)S(1)}, bf16[64,3968]{1,0:T(8,128)(2,1)S(1)}, u32[]{:S(2)}, u32[]{:S(2)}) collective-permute-start(bf16[64,3968]{1,0:T(8,128)(2,1)S(1)} %slice.258), channel_id=1, source_target_pairs={{0,4},{1,5},{2,3},{3,2},{4,0},{5,1},{6,7},{7,6},{8,12},{9,13},{10,... | collective-permute-start | bytes 1523720 | tf_op jit(solution)/shard_map/ppermute | solution.py:478
  400.1 36.8 %collective-permute-start.30 = (bf16[64,3456]{1,0:T(8,128)(2,1)S(1)}, bf16[64,3456]{1,0:T(8,128)(2,1)S(1)}, u32[]{:S(2)}, u32[]{:S(2)}) collective-permute-start(bf16[64,3456]{1,0:T(8,128)(2,1)S(1)} %slice.234), channel_id=1, source_target_pairs={{0,4},{1,5},{2,3},{3,2},{4,0},{5,1},{6,7},{7,6},{8,12},{9,13},{10,... | collective-permute-start | bytes 1327112 | tf_op jit(solution)/shard_map/ppermute | solution.py:478
  414.3 24.8 %collective-permute-start.36 = (bf16[64,3456]{1,0:T(8,128)(2,1)S(1)}, bf16[64,3456]{1,0:T(8,128)(2,1)S(1)}, u32[]{:S(2)}, u32[]{:S(2)}) collective-permute-start(bf16[64,3456]{1,0:T(8,128)(2,1)S(1)} %slice.242), channel_id=1, source_target_pairs={{0,4},{1,5},{2,3},{3,2},{4,0},{5,1},{6,7},{7,6},{8,12},{9,13},{10,... | collective-permute-start | bytes 1327112 | tf_op jit(solution)/shard_map/ppermute | solution.py:478
  (92 other events, 1048.7 us)
